TPU v7x, 32 devices: a whole 2x2x4 slice. The times are simulated.
32 devices in a mesh: gx: 8 (over y, x, core), gy: 4 (over z).
Axes of the slice: x: 2, y: 2, z: 4, core: 2. Of those that a mesh axis runs over, the one named last changes fastest.
Arguments:
- volumes: bfloat16 [2, 64, 256, 1024], P(None, None, 'gy', 'gx'), may hold values from -6 to 6
- peaks: int32 [3, 8, 32], P(None, 'gy', 'gx'), may hold values from -8 to 8
- valid: int32 [8, 32], P('gy', 'gx'), may hold values 0 or 1
Outputs:
- displacement: float32 [3, 8, 32], P(None, 'gy', 'gx')
- peak_score: float32 [8, 32], P('gy', 'gx')
All inputs are finite; a program needn't handle non-finite values. No bound on the sum of `valid` on one device may be relied on, other than what follows from the above.
Results may differ from a plain program's by a relative error of at most 0.0089.
Values may be sent and summed in bfloat16 or wider, within the bound.
A program may use at most 64 MiB of HBM per device.

v0:
```python
import math

import jax
import jax.numpy as jnp
from jax import lax
from jax.sharding import PartitionSpec as P

SWEEPS = 3


def padded_2(array, sides, width):
    for axis, dim in sides:
        devices, length = (lax.axis_size(axis), array.shape[dim])
        up = [(i, (i + 1) % devices) for i in range(devices - 1)]
        down = [(j, i) for i, j in up]
        last = lax.slice_in_dim(array, length - width, length, axis=dim)
        initial = lax.slice_in_dim(array, 0, width, axis=dim)
        before = lax.ppermute(last, axis, up)
        after = lax.ppermute(initial, axis, down)
        array = jnp.concatenate([before, array, after], axis=dim)
    return array


def dft_tables(length):
    counter = jnp.arange(length, dtype=jnp.int32)
    product = counter[:, None] * counter[None, :] % length
    angle = product.astype(jnp.float32) * (2.0 * math.pi / length)
    factor = 1.0 / math.sqrt(length)
    return (
        (jnp.cos(angle) * factor).astype(jnp.bfloat16),
        (jnp.sin(angle) * factor).astype(jnp.bfloat16),
    )


def contract(form, left, table):
    return jnp.einsum(form, left, table, preferred_element_type=jnp.float32)


def spectra(pair, cosine, sine):
    real_one = contract("vzyx,xk->vzyk", pair, cosine).astype(jnp.bfloat16)
    imag_one = (-contract("vzyx,xk->vzyk", pair, sine)).astype(jnp.bfloat16)
    real_two = (
        contract("vzyx,yk->vzkx", real_one, cosine) + contract("vzyx,yk->vzkx", imag_one, sine)
    ).astype(jnp.bfloat16)
    imag_two = (
        contract("vzyx,yk->vzkx", imag_one, cosine) - contract("vzyx,yk->vzkx", real_one, sine)
    ).astype(jnp.bfloat16)
    real_three = contract("vzyx,zk->vkyx", real_two, cosine) + contract(
        "vzyx,zk->vkyx", imag_two, sine
    )
    imag_three = contract("vzyx,zk->vkyx", imag_two, cosine) - contract(
        "vzyx,zk->vkyx", real_two, sine
    )
    return (real_three, imag_three)


def phases(offset, length):
    counter = jnp.arange(length, dtype=jnp.int32)
    shifts = offset + jnp.arange(3, dtype=jnp.int32) - 1
    product = jnp.mod(shifts[:, None] * counter[None, :], length)
    angle = product.astype(jnp.float32) * (2.0 * math.pi / length)
    return (jnp.cos(angle).astype(jnp.bfloat16), jnp.sin(angle).astype(jnp.bfloat16))


def evaluate(real_r, imag_r, peak, length):
    highest = lax.Precision.HIGHEST
    cos_x, sin_x = phases(peak[0], length)
    cos_y, sin_y = phases(peak[1], length)
    cos_z, sin_z = phases(peak[2], length)
    cos_y = cos_y.astype(jnp.float32)
    sin_y = sin_y.astype(jnp.float32)
    cos_z = cos_z.astype(jnp.float32)
    sin_z = sin_z.astype(jnp.float32)
    along_re = contract("zyx,ax->zya", real_r, cos_x) - contract("zyx,ax->zya", imag_r, sin_x)
    along_im = contract("zyx,ax->zya", real_r, sin_x) + contract("zyx,ax->zya", imag_r, cos_x)
    second_re = jnp.einsum("zya,by->zba", along_re, cos_y, precision=highest) - jnp.einsum(
        "zya,by->zba", along_im, sin_y, precision=highest
    )
    second_im = jnp.einsum("zya,by->zba", along_re, sin_y, precision=highest) + jnp.einsum(
        "zya,by->zba", along_im, cos_y, precision=highest
    )
    cube = jnp.einsum("zba,cz->cba", second_re, cos_z, precision=highest) - jnp.einsum(
        "zba,cz->cba", second_im, sin_z, precision=highest
    )
    return cube * (1.0 / (length * math.sqrt(length)))


def block_result(pair, peak, cosine, sine, length):
    real_f, imag_f = spectra(pair, cosine, sine)
    magnitude = (
        jnp.sqrt(real_f[0] * real_f[0] + imag_f[0] * imag_f[0])
        * jnp.sqrt(real_f[1] * real_f[1] + imag_f[1] * imag_f[1])
        + 1.0
    )
    real_r = ((real_f[0] * real_f[1] + imag_f[0] * imag_f[1]) / magnitude).astype(jnp.bfloat16)
    imag_r = ((imag_f[0] * real_f[1] - real_f[0] * imag_f[1]) / magnitude).astype(jnp.bfloat16)
    cube = evaluate(real_r, imag_r, peak, length)
    centre = cube[1, 1, 1]
    lower = jnp.stack([cube[1, 1, 0], cube[1, 0, 1], cube[0, 1, 1]])
    upper = jnp.stack([cube[1, 1, 2], cube[1, 2, 1], cube[2, 1, 1]])
    shift = jnp.tanh((lower - upper) / (jnp.abs(lower + upper - 2.0 * centre) + 0.5))
    return (centre, peak.astype(jnp.float32) + shift)


def relax(padded, data, mask, spacing):
    east = padded[:, 1:-1, 2:]
    west = padded[:, 1:-1, :-2]
    north = padded[:, 2:, 1:-1]
    south = padded[:, :-2, 1:-1]
    north_east = padded[:, 2:, 2:]
    north_west = padded[:, 2:, :-2]
    south_east = padded[:, :-2, 2:]
    south_west = padded[:, :-2, :-2]
    x_xi = spacing + 0.5 * (east[0] - west[0])
    y_xi = 0.5 * (east[1] - west[1])
    x_eta = 0.5 * (north[0] - south[0])
    y_eta = spacing + 0.5 * (north[1] - south[1])
    alpha = x_eta * x_eta + y_eta * y_eta
    beta = x_xi * x_eta + y_xi * y_eta
    gamma = x_xi * x_xi + y_xi * y_xi
    smooth = (
        alpha * (east + west)
        + gamma * (north + south)
        - 0.5 * beta * (north_east - north_west - south_east + south_west)
    ) / (2.0 * (alpha + gamma))
    return smooth + 0.5 * mask * (data - smooth)


def body(volumes, peaks, valid):
    length = volumes.shape[1]
    margin = length // 4
    stride = length // 2
    grid_y = peaks.shape[1]
    grid_x = peaks.shape[2]
    padded = padded_2(volumes, (("gx", 3), ("gy", 2)), margin)
    cosine, sine = dft_tables(length)
    flat_peaks = peaks.reshape(3, grid_y * grid_x).T
    zero = jnp.zeros((), jnp.int32)

    def one_block(index):
        row_index = index // grid_x
        col_index = index % grid_x
        pair = lax.dynamic_slice(
            padded,
            (zero, zero, row_index * stride, col_index * stride),
            (2, length, length, length),
        )
        return block_result(pair, flat_peaks[index], cosine, sine, length)

    scores, data = lax.map(one_block, jnp.arange(grid_y * grid_x, dtype=jnp.int32))
    peak_score = scores.reshape(grid_y, grid_x)
    data = data.T.reshape(3, grid_y, grid_x)
    mask = valid.astype(jnp.float32)
    moved = mask * data
    for sweep_index in range(SWEEPS):
        rimmed = padded_2(moved, (("gx", 2), ("gy", 1)), 1)
        moved = relax(rimmed, data, mask, float(stride))
    return (moved, peak_score)


def solution(mesh):
    return jax.shard_map(
        body,
        mesh=mesh,
        in_specs=(P(None, None, "gy", "gx"), P(None, "gy", "gx"), P("gy", "gx")),
        out_specs=(P(None, "gy", "gx"), P("gy", "gx")),
        check_vma=False,
    )
```

profile of v0, /device:TPU:4, one launch (start us, length us, event | category | flops | bytes accessed | tf_op | source)
XLA Modules:
  0.0 528.0 jit_solution(5321397650685741001)
XLA Ops:
  10.4 4.7 collective-permute-start.1
  34.0 22.1 %collective-permute-done.2 = bf16[2,64,16,160]{3,2,1,0:T(8,128)(2,1)S(1)} collective-permute-done((bf16[2,64,16,160]{3,2,1,0:T(8,128)(2,1)}, bf16[2,64,16,160]{3,2,1,0:T(8,128)(2,1)S(1)}, u32[]{:S(2)}, u32[]{:S(2)}) %collective-permute-start.2) | collective-permute-done | bytes 655392 | tf_op jit(solution)/shard_map/ppermute | solution.py:18
  60.2 9.9 %pad_maximum_fusion.2 = bf16[2,64,96,160]{3,2,1,0:T(8,128)(2,1)} fusion(bf16[2,64,16,160]{3,2,1,0:T(8,128)(2,1)} %collective-permute-done.3, bf16[2,64,64,16]{3,2,1,0:T(8,128)(2,1)} %copy.44, bf16[2,64,64,128]{3,2,1,0:T(8,128)(2,1)S(1)} %copy-done.4, bf16[2,64,64,16]{3,2,1,0:T(8,128)(2,1)} %copy.43, bf16[2,64,16,160]{3,2,1,0:T(8,128)(2,1)S(1)} %collective-permute-done.2), kind=kLoop, calls=%fused_computation.183 | loop fusion | flops 19660800 | bytes 7864320 | tf_op jit(solution)/shard_map/concatenate | solution.py:20
  70.1 410.0 %while.17 = (s32[]{:T(128)}, f32[8]{0:T(128)S(1)}, f32[8,3]{1,0:T(8,128)S(1)}, s32[8]{0:T(128)S(1)}, s32[8,3]{1,0:T(8,128)S(1)}, /*index=5*/bf16[2,64,96,160]{3,...) while((s32[]{:T(128)}, f32[8]{0:T(128)S(1)}, ...), condition=%wide.region_1.2_spmd.clone.clone, body=%wide.region_0.1_spmd.clone.clone.sunk | while | flops 689338240 | bytes 67358016 | solution.py:150
  81.1 4.7 negate_convert_fusion.2
  98.9 4.6 copy.108
  132.3 4.7 negate_convert_fusion.2
  150.2 4.6 copy.108
  183.6 4.7 negate_convert_fusion.2
  201.4 4.6 copy.108
  234.8 4.7 negate_convert_fusion.2
  252.7 4.6 copy.108
  286.1 4.7 negate_convert_fusion.2
  303.9 4.6 copy.108
  337.3 4.7 negate_convert_fusion.2
  355.2 4.6 copy.108
  388.6 4.7 negate_convert_fusion.2
  406.4 4.6 copy.108
  439.8 4.7 negate_convert_fusion.2
  457.7 4.6 copy.108
  482.9 4.5 collective-permute-start.5
  490.1 4.5 collective-permute-start.7
  505.4 4.8 collective-permute-start.11
  521.0 4.8 collective-permute-start.15
  (448 shorter events, 358.9 us)
Async XLA Ops:
  7.0 12.3 %collective-permute-start = (bf16[2,64,64,16]{2,3,1,0:T(8,128)(2,1)S(1)}, bf16[2,64,64,16]{2,3,1,0:T(8,128)(2,1)S(1)}, u32[]{:S(2)}, u32[]{:S(2)}) collective-permute-start(bf16[2,64,64,16]{2,3,1,0:T(8,128)(2,1)S(1)} %copy.73), channel_id=1, source_target_pairs={{0,4},{4,8},{8,12},{12,16},{16,20},{20,24},{24,28},{1,5},{5,9},{9,... | collective-permute-start | bytes 786440 | tf_op jit(solution)/shard_map/ppermute | solution.py:18
  10.4 14.4 %copy-start.4 = (bf16[2,64,64,128]{3,2,1,0:T(8,128)(2,1)S(1)}, bf16[2,64,64,128]{3,2,1,0:T(8,128)(2,1)}, u32[]{:S(2)}) copy-start(bf16[2,64,64,128]{3,2,1,0:T(8,128)(2,1)} %param.5) | copy-start | bytes 6291460
  10.4 11.8 %collective-permute-start.1 = (bf16[2,64,64,16]{2,3,1,0:T(8,128)(2,1)}, bf16[2,64,64,16]{2,3,1,0:T(8,128)(2,1)}, u32[]{:S(2)}, u32[]{:S(2)}) collective-permute-start(bf16[2,64,64,16]{2,3,1,0:T(8,128)(2,1)} %copy.74), channel_id=1, source_target_pairs={{4,0},{8,4},{12,8},{16,12},{20,16},{24,20},{28,24},{5,1},{9,5},{13... | collective-permute-start | bytes 786440 | tf_op jit(solution)/shard_map/ppermute | solution.py:19
  24.8 8.9 %copy-start.5 = (s32[2,4]{1,0:T(2,128)S(1)}, s32[2,4]{1,0:T(2,128)}, u32[]{:S(2)}) copy-start(s32[2,4]{1,0:T(2,128)} %param.7) | copy-start | bytes 100
  24.8 9.0 %copy-start.6 = (s32[3,2,4]{2,1,0:T(2,128)S(1)}, s32[3,2,4]{2,1,0:T(2,128)}, u32[]{:S(2)}) copy-start(s32[3,2,4]{2,1,0:T(2,128)} %param.6) | copy-start | bytes 292
  28.9 27.1 %collective-permute-start.2 = (bf16[2,64,16,160]{3,2,1,0:T(8,128)(2,1)}, bf16[2,64,16,160]{3,2,1,0:T(8,128)(2,1)S(1)}, u32[]{:S(2)}, u32[]{:S(2)}) collective-permute-start(bf16[2,64,16,160]{3,2,1,0:T(8,128)(2,1)} %get-tuple-element.267), channel_id=1, source_target_pairs={{0,1},{1,2},{2,3},{4,5},{5,6},{6,7},{8,9},{9,10},{10,11},{12,13},{... | collective-permute-start | bytes 1966088 | tf_op jit(solution)/shard_map/ppermute | solution.py:18
  32.5 27.8 %collective-permute-start.3 = (bf16[2,64,16,160]{3,2,1,0:T(8,128)(2,1)}, bf16[2,64,16,160]{3,2,1,0:T(8,128)(2,1)}, u32[]{:S(2)}, u32[]{:S(2)}) collective-permute-start(bf16[2,64,16,160]{3,2,1,0:T(8,128)(2,1)} %get-tuple-element.268), channel_id=1, source_target_pairs={{1,0},{2,1},{3,2},{5,4},{6,5},{7,6},{9,8},{10,9},{11,10},{13,12},{... | collective-permute-start | bytes 1966088 | tf_op jit(solution)/shard_map/ppermute | solution.py:19
  81.0 6.9 %copy-start.3 = (bf16[2,64,64,64]{3,2,1,0:T(8,128)(2,1)}, bf16[2,64,64,64]{3,2,1,0:T(8,128)(2,1)S(1)}, u32[]{:S(2)}) copy-start(bf16[2,64,64,64]{3,2,1,0:T(8,128)(2,1)S(1)} %convolution_convert_fusion.2) | copy-start | bytes 3145732 | tf_op jit(solution)/shard_map/while
  132.3 6.9 %copy-start.3 = (bf16[2,64,64,64]{3,2,1,0:T(8,128)(2,1)}, bf16[2,64,64,64]{3,2,1,0:T(8,128)(2,1)S(1)}, u32[]{:S(2)}) copy-start(bf16[2,64,64,64]{3,2,1,0:T(8,128)(2,1)S(1)} %convolution_convert_fusion.2) | copy-start | bytes 3145732 | tf_op jit(solution)/shard_map/while
  183.6 6.9 %copy-start.3 = (bf16[2,64,64,64]{3,2,1,0:T(8,128)(2,1)}, bf16[2,64,64,64]{3,2,1,0:T(8,128)(2,1)S(1)}, u32[]{:S(2)}) copy-start(bf16[2,64,64,64]{3,2,1,0:T(8,128)(2,1)S(1)} %convolution_convert_fusion.2) | copy-start | bytes 3145732 | tf_op jit(solution)/shard_map/while
  234.8 6.9 %copy-start.3 = (bf16[2,64,64,64]{3,2,1,0:T(8,128)(2,1)}, bf16[2,64,64,64]{3,2,1,0:T(8,128)(2,1)S(1)}, u32[]{:S(2)}) copy-start(bf16[2,64,64,64]{3,2,1,0:T(8,128)(2,1)S(1)} %convolution_convert_fusion.2) | copy-start | bytes 3145732 | tf_op jit(solution)/shard_map/while
  388.6 6.9 %copy-start.3 = (bf16[2,64,64,64]{3,2,1,0:T(8,128)(2,1)}, bf16[2,64,64,64]{3,2,1,0:T(8,128)(2,1)S(1)}, u32[]{:S(2)}) copy-start(bf16[2,64,64,64]{3,2,1,0:T(8,128)(2,1)S(1)} %convolution_convert_fusion.2) | copy-start | bytes 3145732 | tf_op jit(solution)/shard_map/while
  480.9 6.5 %collective-permute-start.4 = (f32[3,2,1]{2,1,0:T(2,128)S(1)}, f32[3,2,1]{2,1,0:T(2,128)S(1)}, u32[]{:S(2)}, u32[]{:S(2)}) collective-permute-start(f32[3,2,1]{2,1,0:T(2,128)S(1)} %get-tuple-element.293), channel_id=1, source_target_pairs={{0,4},{4,8},{8,12},{12,16},{16,20},{20,24},{24,28},{1,5},{5,9},{9,... | collective-permute-start | bytes 80 | tf_op jit(solution)/shard_map/ppermute | solution.py:18
  482.9 5.8 %collective-permute-start.5 = (f32[3,2,1]{2,1,0:T(2,128)S(1)}, f32[3,2,1]{2,1,0:T(2,128)S(1)}, u32[]{:S(2)}, u32[]{:S(2)}) collective-permute-start(f32[3,2,1]{2,1,0:T(2,128)S(1)} %get-tuple-element.294), channel_id=1, source_target_pairs={{4,0},{8,4},{12,8},{16,12},{20,16},{24,20},{28,24},{5,1},{9,5},{13... | collective-permute-start | bytes 80 | tf_op jit(solution)/shard_map/ppermute | solution.py:19
  488.8 5.9 %collective-permute-start.6 = (f32[3,1,6]{2,1,0:T(1,128)S(1)}, f32[3,1,6]{2,1,0:T(1,128)S(1)}, u32[]{:S(2)}, u32[]{:S(2)}) collective-permute-start(f32[3,1,6]{2,1,0:T(1,128)S(1)} %get-tuple-element.291), channel_id=1, source_target_pairs={{1,0},{2,1},{3,2},{5,4},{6,5},{7,6},{9,8},{10,9},{11,10},{13,12},{... | collective-permute-start | bytes 224 | tf_op jit(solution)/shard_map/ppermute | solution.py:19
  490.1 5.8 %collective-permute-start.7 = (f32[3,1,6]{2,1,0:T(1,128)S(1)}, f32[3,1,6]{2,1,0:T(1,128)S(1)}, u32[]{:S(2)}, u32[]{:S(2)}) collective-permute-start(f32[3,1,6]{2,1,0:T(1,128)S(1)} %get-tuple-element.292), channel_id=1, source_target_pairs={{0,1},{1,2},{2,3},{4,5},{5,6},{6,7},{8,9},{9,10},{10,11},{12,13},{... | collective-permute-start | bytes 224 | tf_op jit(solution)/shard_map/ppermute | solution.py:18
  496.3 6.5 %collective-permute-start.8 = (f32[3,2,1]{2,1,0:T(2,128)S(1)}, f32[3,2,1]{2,1,0:T(2,128)S(1)}, u32[]{:S(2)}, u32[]{:S(2)}) collective-permute-start(f32[3,2,1]{2,1,0:T(2,128)S(1)} %get-tuple-element.289), channel_id=1, source_target_pairs={{0,4},{4,8},{8,12},{12,16},{16,20},{20,24},{24,28},{1,5},{5,9},{9,... | collective-permute-start | bytes 80 | tf_op jit(solution)/shard_map/ppermute | solution.py:18
  498.2 5.8 %collective-permute-start.9 = (f32[3,2,1]{2,1,0:T(2,128)S(1)}, f32[3,2,1]{2,1,0:T(2,128)S(1)}, u32[]{:S(2)}, u32[]{:S(2)}) collective-permute-start(f32[3,2,1]{2,1,0:T(2,128)S(1)} %get-tuple-element.290), channel_id=1, source_target_pairs={{4,0},{8,4},{12,8},{16,12},{20,16},{24,20},{28,24},{5,1},{9,5},{13... | collective-permute-start | bytes 80 | tf_op jit(solution)/shard_map/ppermute | solution.py:19
  504.1 6.2 %collective-permute-start.10 = (f32[3,1,6]{2,1,0:T(1,128)S(1)}, f32[3,1,6]{2,1,0:T(1,128)S(1)}, u32[]{:S(2)}, u32[]{:S(2)}) collective-permute-start(f32[3,1,6]{2,1,0:T(1,128)S(1)} %get-tuple-element.287), channel_id=1, source_target_pairs={{1,0},{2,1},{3,2},{5,4},{6,5},{7,6},{9,8},{10,9},{11,10},{13,12},{... | collective-permute-start | bytes 224 | tf_op jit(solution)/shard_map/ppermute | solution.py:19
  505.4 6.1 %collective-permute-start.11 = (f32[3,1,6]{2,1,0:T(1,128)S(1)}, f32[3,1,6]{2,1,0:T(1,128)S(1)}, u32[]{:S(2)}, u32[]{:S(2)}) collective-permute-start(f32[3,1,6]{2,1,0:T(1,128)S(1)} %get-tuple-element.288), channel_id=1, source_target_pairs={{0,1},{1,2},{2,3},{4,5},{5,6},{6,7},{8,9},{9,10},{10,11},{12,13},{... | collective-permute-start | bytes 224 | tf_op jit(solution)/shard_map/ppermute | solution.py:18
  511.9 6.5 %collective-permute-start.12 = (f32[3,2,1]{2,1,0:T(2,128)S(1)}, f32[3,2,1]{2,1,0:T(2,128)S(1)}, u32[]{:S(2)}, u32[]{:S(2)}) collective-permute-start(f32[3,2,1]{2,1,0:T(2,128)S(1)} %get-tuple-element.285), channel_id=1, source_target_pairs={{0,4},{4,8},{8,12},{12,16},{16,20},{20,24},{24,28},{1,5},{5,9},{9,... | collective-permute-start | bytes 80 | tf_op jit(solution)/shard_map/ppermute | solution.py:18
  513.8 5.8 %collective-permute-start.13 = (f32[3,2,1]{2,1,0:T(2,128)S(1)}, f32[3,2,1]{2,1,0:T(2,128)S(1)}, u32[]{:S(2)}, u32[]{:S(2)}) collective-permute-start(f32[3,2,1]{2,1,0:T(2,128)S(1)} %get-tuple-element.286), channel_id=1, source_target_pairs={{4,0},{8,4},{12,8},{16,12},{20,16},{24,20},{28,24},{5,1},{9,5},{13... | collective-permute-start | bytes 80 | tf_op jit(solution)/shard_map/ppermute | solution.py:19
  519.8 6.2 %collective-permute-start.14 = (f32[3,1,6]{2,1,0:T(1,128)S(1)}, f32[3,1,6]{2,1,0:T(1,128)S(1)}, u32[]{:S(2)}, u32[]{:S(2)}) collective-permute-start(f32[3,1,6]{2,1,0:T(1,128)S(1)} %get-tuple-element.283), channel_id=1, source_target_pairs={{1,0},{2,1},{3,2},{5,4},{6,5},{7,6},{9,8},{10,9},{11,10},{13,12},{... | collective-permute-start | bytes 224 | tf_op jit(solution)/shard_map/ppermute | solution.py:19
  521.0 6.1 %collective-permute-start.15 = (f32[3,1,6]{2,1,0:T(1,128)S(1)}, f32[3,1,6]{2,1,0:T(1,128)S(1)}, u32[]{:S(2)}, u32[]{:S(2)}) collective-permute-start(f32[3,1,6]{2,1,0:T(1,128)S(1)} %get-tuple-element.284), channel_id=1, source_target_pairs={{0,1},{1,2},{2,3},{4,5},{5,6},{6,7},{8,9},{9,10},{10,11},{12,13},{... | collective-permute-start | bytes 224 | tf_op jit(solution)/shard_map/ppermute | solution.py:18
  (27 other events, 64.8 us)
where the time goes:
time: 534 us; the launch traced here: 528 us
  matrix products  194 us (36%)
  local copies, waits for them, and re-layouts  125 us (23%)
  other arithmetic  82 us (15%)
  starting transfers between devices  48.8 us (9%)
  waiting for transfers between devices  39 us (7%)
  loops' own time  38.6 us (7%)
    dot_general x112, matrix products, contract(): return jnp.einsum(form, left, table, preferred_element_type=jnp.float32)  182 us
    another operation x1, loops' own time, body(): lax.map(one_block, jnp.arange(grid_y * grid_x, dtype=jnp.int32))  38.6 us
    convert_element_type x8, local copies, waits for them, and re-layouts, spectra(): real_two = (contract('vzyx,yk->vzkx', real_one, cosine) + contract('vzyx,...  36.8 us
    add x8, other arithmetic, block_result(): return (centre, peak.astype(jnp.float32) + shift)  31.4 us
    convert_element_type x8, local copies, waits for them, and re-layouts, spectra(): imag_two = (contract('vzyx,yk->vzkx', imag_one, cosine) - contract('vzyx,...  30.9 us
    ppermute x8, waiting for transfers between devices, padded_2(): before = lax.ppermute(last, axis, up)  29.9 us
    ppermute x8, starting transfers between devices, padded_2(): before = lax.ppermute(last, axis, up)  25.4 us
    ppermute x8, starting transfers between devices, padded_2(): after = lax.ppermute(initial, axis, down)  23.4 us
  transfers between devices with their start and end apart: 16, of which 10 were waited for; matrix products, arithmetic and copies ran while one was open for 1% of the time, Pallas kernels for 0%

commit v1 on v0

v1 whole, which is shorter than its diff:
```python
import functools
import math

import jax
import jax.numpy as jnp
import ml_dtypes
import numpy as np
from jax import lax
from jax.experimental import pallas as pl
from jax.experimental.pallas import tpu as pltpu
from jax.sharding import PartitionSpec as P

SWEEPS = 3
ZSTEP = 4


def padded_2(array, sides, width):
    for axis, dim in sides:
        devices, length = (lax.axis_size(axis), array.shape[dim])
        up = [(i, (i + 1) % devices) for i in range(devices - 1)]
        down = [(j, i) for i, j in up]
        last = lax.slice_in_dim(array, length - width, length, axis=dim)
        initial = lax.slice_in_dim(array, 0, width, axis=dim)
        before = lax.ppermute(last, axis, up)
        after = lax.ppermute(initial, axis, down)
        array = jnp.concatenate([before, array, after], axis=dim)
    return array


def tables(length, grid_x, grid_y):
    counter = np.arange(length)
    angle = (counter[:, None] * counter[None, :] % length).astype(np.float32) * np.float32(
        2.0 * math.pi / length
    )
    factor = np.float32(1.0 / math.sqrt(length))
    cosine = (np.cos(angle) * factor).astype(ml_dtypes.bfloat16)
    sine = (np.sin(angle) * factor).astype(ml_dtypes.bfloat16)
    stride = length // 2
    half = length // 2 + 1
    width = stride * grid_x + stride
    height = stride * grid_y + stride
    along_x = np.zeros((width, 2, grid_x, length), ml_dtypes.bfloat16)
    for i in range(grid_x):
        along_x[i * stride : i * stride + length, 0, i] = cosine
        along_x[i * stride : i * stride + length, 1, i] = -sine
    lines = grid_y * half
    padded = -(-lines // 8) * 8
    along_y = np.zeros((2, padded, 2, height), ml_dtypes.bfloat16)
    for j in range(grid_y):
        rows = slice(j * half, (j + 1) * half)
        window = slice(j * stride, j * stride + length)
        along_y[0, rows, 0, window] = cosine[:half]
        along_y[0, rows, 1, window] = sine[:half]
        along_y[1, rows, 0, window] = -sine[:half]
        along_y[1, rows, 1, window] = cosine[:half]
    along_z = np.block([[cosine, sine], [-sine, cosine]])
    return (
        along_x.reshape(width, 2 * grid_x * length),
        along_y.reshape(2 * padded, 2 * height),
        along_z,
    )


def spectrum_kernel(
    grid_x, grid_y, vol, table_x, table_y, table_z, table_e, cos_y, sin_y, out, first, second
):
    length = vol.shape[1]
    height = vol.shape[2]
    half = length // 2 + 1
    lanes = grid_x * length
    padded = table_y.shape[0] // 2
    pieces = 2 * lanes // 128

    def slab(step, carry):
        z0 = step * ZSTEP
        for v in range(2):
            rows = vol[v, pl.ds(z0, ZSTEP)].reshape(ZSTEP * height, vol.shape[3])
            one = jnp.dot(rows, table_x[...], preferred_element_type=jnp.float32)
            first[v] = one.astype(jnp.bfloat16)
        for i in range(ZSTEP):
            ys = slice(i * height, (i + 1) * height)
            right = jnp.concatenate(
                [
                    jnp.concatenate([first[0, ys, :lanes], first[1, ys, :lanes]], axis=1),
                    jnp.concatenate([first[0, ys, lanes:], first[1, ys, lanes:]], axis=1),
                ],
                axis=0,
            )
            two = jnp.dot(table_y[...], right, preferred_element_type=jnp.float32)
            for c in range(2):
                for t in range(pieces):
                    second[t, pl.ds(c * length + z0 + i, padded, stride=2 * length), :] = two[
                        c * padded : (c + 1) * padded, t * 128 : (t + 1) * 128
                    ]
        return carry

    lax.fori_loop(0, length // ZSTEP, slab, 0)

    group = lax.broadcasted_iota(jnp.int32, (8, lanes), 1) // length

    for j in range(grid_y):

        def line(ky, sums):
            base = pl.multiple_of((j * half + ky) * 2 * length, 2 * length)
            right = jnp.concatenate(
                [second[t, pl.ds(base, 2 * length), :].astype(jnp.bfloat16) for t in range(pieces)],
                axis=1,
            )
            three = jnp.dot(table_z[...], right, preferred_element_type=jnp.float32)
            re1, im1 = three[:length, :lanes], three[length:, :lanes]
            re2, im2 = three[:length, lanes:], three[length:, lanes:]
            size = (re1 * re1 + im1 * im1) * (re2 * re2 + im2 * im2)
            scale = 1.0 / (jnp.sqrt(size) + 1.0)
            real_r = ((re1 * re2 + im1 * im2) * scale).astype(jnp.bfloat16)
            imag_r = ((im1 * re2 - re1 * im2) * scale).astype(jnp.bfloat16)
            both = jnp.concatenate([real_r, imag_r], axis=0)
            along = jnp.dot(table_e[j], both, preferred_element_type=jnp.float32)
            own = along[:8]
            for i in range(1, grid_x):
                own = jnp.where(group == i, along[8 * i : 8 * i + 8], own)
            new = []
            for o in range(3):
                new.append(sums[2 * o] + own * cos_y[j, o, pl.ds(ky, 1), :])
                new.append(sums[2 * o + 1] + own * sin_y[j, o, pl.ds(ky, 1), :])
            return tuple(new)

        zero = jnp.zeros((8, lanes), jnp.float32)
        sums = lax.fori_loop(0, half, line, (zero,) * 6)
        for n in range(6):
            out[j, n] = sums[n]


def phases(offset, length):
    counter = jnp.arange(length, dtype=jnp.int32)
    shifts = offset[..., None] + jnp.arange(3, dtype=jnp.int32) - 1
    product = jnp.mod(shifts[..., None] * counter, length)
    angle = product.astype(jnp.float32) * (2.0 * math.pi / length)
    return (jnp.cos(angle).astype(jnp.bfloat16), jnp.sin(angle).astype(jnp.bfloat16))


def relax(padded, data, mask, spacing):
    east = padded[:, 1:-1, 2:]
    west = padded[:, 1:-1, :-2]
    north = padded[:, 2:, 1:-1]
    south = padded[:, :-2, 1:-1]
    north_east = padded[:, 2:, 2:]
    north_west = padded[:, 2:, :-2]
    south_east = padded[:, :-2, 2:]
    south_west = padded[:, :-2, :-2]
    x_xi = spacing + 0.5 * (east[0] - west[0])
    y_xi = 0.5 * (east[1] - west[1])
    x_eta = 0.5 * (north[0] - south[0])
    y_eta = spacing + 0.5 * (north[1] - south[1])
    alpha = x_eta * x_eta + y_eta * y_eta
    beta = x_xi * x_eta + y_xi * y_eta
    gamma = x_xi * x_xi + y_xi * y_xi
    smooth = (
        alpha * (east + west)
        + gamma * (north + south)
        - 0.5 * beta * (north_east - north_west - south_east + south_west)
    ) / (2.0 * (alpha + gamma))
    return smooth + 0.5 * mask * (data - smooth)


def body(volumes, peaks, valid):
    length = volumes.shape[1]
    margin = length // 4
    stride = length // 2
    half = length // 2 + 1
    _, grid_y, grid_x = peaks.shape
    lanes = grid_x * length
    padded = padded_2(volumes, (("gx", 3), ("gy", 2)), margin)
    table_x, table_y, table_z = tables(length, grid_x, grid_y)
    cosine, sine = phases(peaks, length)
    cos_z, sin_z = cosine[2], sine[2]
    rows_re = jnp.concatenate([cos_z, -sin_z], axis=-1)
    rows_im = jnp.concatenate([sin_z, cos_z], axis=-1)
    table_e = jnp.stack([rows_re, rows_im], axis=3).reshape(grid_y, grid_x, 6, 2 * length)
    table_e = jnp.pad(table_e, ((0, 0), (0, 0), (0, 2), (0, 0))).reshape(
        grid_y, grid_x * 8, 2 * length
    )
    weight = np.full((half,), 2.0, np.float32)
    weight[0] = weight[-1] = 1.0

    def spread(table):
        table = table[..., :half].astype(jnp.float32) * weight
        table = jnp.broadcast_to(
            table.transpose(0, 2, 3, 1)[..., None], (grid_y, 3, half, grid_x, length)
        )
        return table.reshape(grid_y, 3, half, lanes)

    sums = pl.pallas_call(
        functools.partial(spectrum_kernel, grid_x, grid_y),
        out_shape=jax.ShapeDtypeStruct((grid_y, 6, 8, lanes), jnp.float32),
        in_specs=[pl.BlockSpec(memory_space=pltpu.VMEM)] * 7,
        out_specs=pl.BlockSpec(memory_space=pltpu.VMEM),
        scratch_shapes=[
            pltpu.VMEM((2, ZSTEP * padded.shape[2], 2 * lanes), jnp.bfloat16),
            pltpu.VMEM((2 * lanes // 128, table_y.shape[0] * length, 128), jnp.float32),
        ],
        compiler_params=pltpu.CompilerParams(vmem_limit_bytes=56 * 1024 * 1024),
        name="spectrum",
    )(padded, table_x, table_y, table_z, table_e, spread(cosine[1]), spread(sine[1]))

    sums = sums.reshape(grid_y, 3, 2, 8, grid_x, length)
    factor = 1.0 / (length * math.sqrt(length))
    cos_x = cosine[0].astype(jnp.float32) * factor
    sin_x = sine[0].astype(jnp.float32) * factor

    def corr(ox, oy, oz):
        real = sums[:, oy, 0, 2 * oz] - sums[:, oy, 1, 2 * oz + 1]
        imag = sums[:, oy, 1, 2 * oz] + sums[:, oy, 0, 2 * oz + 1]
        return jnp.sum(real * cos_x[:, :, ox] - imag * sin_x[:, :, ox], axis=-1)

    centre = corr(1, 1, 1)
    lower = jnp.stack([corr(0, 1, 1), corr(1, 0, 1), corr(1, 1, 0)])
    upper = jnp.stack([corr(2, 1, 1), corr(1, 2, 1), corr(1, 1, 2)])
    shift = jnp.tanh((lower - upper) / (jnp.abs(lower + upper - 2.0 * centre) + 0.5))
    data = peaks.astype(jnp.float32) + shift
    mask = valid.astype(jnp.float32)
    moved = mask * data
    for _ in range(SWEEPS):
        rimmed = padded_2(moved, (("gx", 2), ("gy", 1)), 1)
        moved = relax(rimmed, data, mask, float(stride))
    return (moved, centre)


def solution(mesh):
    return jax.shard_map(
        body,
        mesh=mesh,
        in_specs=(P(None, None, "gy", "gx"), P(None, "gy", "gx"), P("gy", "gx")),
        out_specs=(P(None, "gy", "gx"), P("gy", "gx")),
        check_vma=False,
    )
```

time: 534 us -> 165 us (0.31)
  matrix products: 194 us -> 0 us
  local copies, waits for them, and re-layouts: 125 us -> 17.2 us
  other arithmetic: 82 us -> 14.9 us
  Pallas kernels: 0 us -> 49.5 us
  loops' own time: 38.6 us -> 0 us
  starting transfers between devices: 48.8 us -> 42 us
    dot_general x160 -> x0, matrix products: 194 us -> none  [the longest x112 182 us: contract(): return jnp.einsum(form, left, table, preferred_element_type=jnp.float32)]
    convert_element_type x16 -> x0, local copies, waits for them, and re-layouts: 67.7 us -> none  [the longest x8 36.8 us: spectra(): real_two = (contract('vzyx,yk->vzkx', real_one, cosine) + contract('vzyx,...]
    pallas_call x0 -> x1, Pallas kernels: none -> 49.5 us  [body(): pl.pallas_call(functools.partial(spectrum_kernel, grid_x, grid_y), out_sh...]
    another operation x1 -> x0, loops' own time: 38.6 us -> none  [body(): lax.map(one_block, jnp.arange(grid_y * grid_x, dtype=jnp.int32))]
    add x16 -> x0, other arithmetic: 31.7 us -> none  [the longest x8 31.4 us: block_result(): return (centre, peak.astype(jnp.float32) + shift)]
    convert_element_type x8 -> x1, other arithmetic: 18.3 us -> 0.35 us  [phases(): jnp.cos(angle).astype(jnp.bfloat16)]
    while x64 -> x0, local copies, waits for them, and re-layouts: 16.7 us -> none
    sub x32 -> x1, other arithmetic: 16.1 us -> 0.01 us  [phases(): shifts = offset[..., None] + jnp.arange(3, dtype=jnp.int32) - 1]
  transfers between devices with their start and end apart: 16 -> 16, of which waited for: 10 -> 10; matrix products, arithmetic and copies ran while one was open for 1% -> 5% of each run, Pallas kernels for 0% -> 0%
where the time goes in v1:
time: 165 us; the launch traced here: 163 us
  Pallas kernels  49.5 us (30%)
  starting transfers between devices  42 us (25%)
  waiting for transfers between devices  38.6 us (23%)
  local copies, waits for them, and re-layouts  17.2 us (10%)
  other arithmetic  14.9 us (9%)
    pallas_call x1, Pallas kernels, body(): pl.pallas_call(functools.partial(spectrum_kernel, grid_x, grid_y), out_sh...  49.5 us
    ppermute x8, starting transfers between devices, padded_2(): before = lax.ppermute(last, axis, up)  28.3 us
    ppermute x8, waiting for transfers between devices, padded_2(): after = lax.ppermute(initial, axis, down)  20.5 us
    ppermute x8, waiting for transfers between devices, padded_2(): before = lax.ppermute(last, axis, up)  18.1 us
    ppermute x8, starting transfers between devices, padded_2(): after = lax.ppermute(initial, axis, down)  13.7 us
    concatenate x7, other arithmetic, padded_2(): array = jnp.concatenate([before, array, after], axis=dim)  9.18 us
    slice x4, local copies, waits for them, and re-layouts, padded_2(): last = lax.slice_in_dim(array, length - width, length, axis=dim)  4.67 us
    unnamed x18, local copies, waits for them, and re-layouts  3.55 us
  transfers between devices with their start and end apart: 16, of which 10 were waited for; matrix products, arithmetic and copies ran while one was open for 5% of the time, Pallas kernels for 0%

profile of v1, /device:TPU:4, one launch (start us, length us, event | category | flops | bytes accessed | tf_op | source)
XLA Modules:
  0.0 163.1 jit_solution(16748680718774427915)
XLA Ops:
  0.6 4.5 %fusion.106 = (bf16[2,64,64,16]{3,2,1,0:T(8,128)(2,1)S(1)}, bf16[2,64,64,16]{3,2,1,0:T(8,128)(2,1)}) fusion(bf16[2,64,64,128]{3,2,1,0:T(8,128)(2,1)} %param.7), kind=kLoop, calls=%fused_computation.219 | loop fusion | bytes 1048576 | tf_op jit(solution)/shard_map/slice | solution.py:22
  5.1 2.0 %copy.99 = bf16[2,64,64,16]{2,3,1,0:T(8,128)(2,1)S(1)} copy(bf16[2,64,64,16]{3,2,1,0:T(8,128)(2,1)} %get-tuple-element.31) | data formatting | bytes 524288
  7.1 2.8 %collective-permute-start.1 = (bf16[2,64,64,16]{2,3,1,0:T(8,128)(2,1)S(1)}, bf16[2,64,64,16]{2,3,1,0:T(8,128)(2,1)S(1)}, u32[]{:S(2)}, u32[]{:S(2)}) collective-permute-start(bf16[2,64,64,16]{2,3,1,0:T(8,128)(2,1)S(1)} %copy.99), channel_id=1, source_target_pairs={{4,0},{8,4},{12,8},{16,12},{20,16},{24,20},{28,24},{5,1},{9,5},{13... | collective-permute-start | bytes 786440 | tf_op jit(solution)/shard_map/ppermute | solution.py:25
  11.4 1.9 %collective-permute-start = (bf16[2,64,64,16]{2,3,1,0:T(8,128)(2,1)}, bf16[2,64,64,16]{2,3,1,0:T(8,128)(2,1)}, u32[]{:S(2)}, u32[]{:S(2)}) collective-permute-start(bf16[2,64,64,16]{2,3,1,0:T(8,128)(2,1)} %copy.98), channel_id=1, source_target_pairs={{0,4},{4,8},{8,12},{12,16},{16,20},{20,24},{24,28},{1,5},{5,9},{9,... | collective-permute-start | bytes 786440 | tf_op jit(solution)/shard_map/ppermute | solution.py:24
  18.4 1.8 %copy.65 = bf16[2,64,64,16]{3,2,1,0:T(8,128)(2,1)} copy(bf16[2,64,64,16]{2,3,1,0:T(8,128)(2,1)S(1)} %collective-permute-done.1) | data formatting | bytes 524288 | tf_op jit(solution)/shard_map/ppermute | solution.py:25
  20.1 3.1 %collective-permute-done = bf16[2,64,64,16]{2,3,1,0:T(8,128)(2,1)} collective-permute-done((bf16[2,64,64,16]{2,3,1,0:T(8,128)(2,1)}, bf16[2,64,64,16]{2,3,1,0:T(8,128)(2,1)}, u32[]{:S(2)}, u32[]{:S(2)}) %collective-permute-start) | collective-permute-done | bytes 262176 | tf_op jit(solution)/shard_map/ppermute | solution.py:24
  23.3 2.6 %copy.64 = bf16[2,64,64,16]{3,2,1,0:T(8,128)(2,1)} copy(bf16[2,64,64,16]{2,3,1,0:T(8,128)(2,1)} %collective-permute-done) | data formatting | bytes 524288 | tf_op jit(solution)/shard_map/ppermute | solution.py:24
  25.9 2.9 %pad_maximum_fusion.3 = (bf16[2,64,16,160]{3,2,1,0:T(8,128)(2,1)S(1)}, bf16[2,64,16,160]{3,2,1,0:T(8,128)(2,1)S(1)}) fusion(bf16[2,64,64,16]{3,2,1,0:T(8,128)(2,1)} %copy.65, bf16[2,64,64,128]{3,2,1,0:T(8,128)(2,1)S(1)} %copy-done, bf16[2,64,64,16]{3,2,1,0:T(8,128)(2,1)} %copy.64), kind=kLoop, calls=%fused_computation.3 | loop fusion | flops 3932160 | bytes 3932160 | tf_op jit(solution)/shard_map/slice | solution.py:22
  30.1 4.6 %collective-permute-start.2 = (bf16[2,64,16,160]{3,2,1,0:T(8,128)(2,1)S(1)}, bf16[2,64,16,160]{3,2,1,0:T(8,128)(2,1)S(1)}, u32[]{:S(2)}, u32[]{:S(2)}) collective-permute-start(bf16[2,64,16,160]{3,2,1,0:T(8,128)(2,1)S(1)} %get-tuple-element.28), channel_id=1, source_target_pairs={{0,1},{1,2},{2,3},{4,5},{5,6},{6,7},{8,9},{9,10},{10,11},{12,13},{... | collective-permute-start | bytes 1966088 | tf_op jit(solution)/shard_map/ppermute | solution.py:24
  34.9 19.9 %collective-permute-done.3 = bf16[2,64,16,160]{3,2,1,0:T(8,128)(2,1)S(1)} collective-permute-done((bf16[2,64,16,160]{3,2,1,0:T(8,128)(2,1)S(1)}, bf16[2,64,16,160]{3,2,1,0:T(8,128)(2,1)S(1)}, u32[]{:S(2)}, u32[]{:S(2)}) %collective-permute-start.3) | collective-permute-done | bytes 655392 | tf_op jit(solution)/shard_map/ppermute | solution.py:25
  56.1 8.7 %pad_maximum_fusion.vol = bf16[2,64,96,160]{3,2,1,0:T(8,128)(2,1)} fusion(bf16[2,64,16,160]{3,2,1,0:T(8,128)(2,1)S(1)} %collective-permute-done.3, bf16[2,64,64,16]{3,2,1,0:T(8,128)(2,1)S(1)} %copy-done.1, bf16[2,64,64,128]{3,2,1,0:T(8,128)(2,1)S(1)} %copy-done, bf16[2,64,64,16]{3,2,1,0:T(8,128)(2,1)S(1)} %copy-done.2, ...), kind=kLoop, calls=%fused_computation | loop fusion | flops 19660800 | bytes 7864320 | tf_op jit(solution)/shard_map/concatenate | solution.py:26
  64.7 49.5 %spectrum.1 = f32[2,6,8,256]{3,2,1,0:T(8,128)} custom-call(bf16[2,64,96,160]{3,2,1,0:T(8,128)(2,1)} %pad_maximum_fusion.vol, bf16[160,512]{1,0:T(8,128)(2,1)} %constant.43.clone.table_x, bf16[144,192]{1,0:T(8,128)(2,1)} %constant.44.clone.table_y, bf16[128,128]{1,0:T(8,128)(2,1)} %constant.45.clone.table_z, bf16[2,32,128]{2,1,0:T(8,128)(2,1)} %pad_bitcast_fusion.table_e, ...), custom_call_target="tpu_custom_call" | custom-call | tf_op jit(solution)/shard_map/spectrum/pallas_call | solution.py:192
  115.6 2.0 %collective-permute-start.5 = (f32[3,2,1]{2,1,0:T(2,128)S(1)}, f32[3,2,1]{2,1,0:T(2,128)S(1)}, u32[]{:S(2)}, u32[]{:S(2)}) collective-permute-start(f32[3,2,1]{2,1,0:T(2,128)S(1)} %get-tuple-element.61), channel_id=1, source_target_pairs={{4,0},{8,4},{12,8},{16,12},{20,16},{24,20},{28,24},{5,1},{9,5},{13... | collective-permute-start | bytes 80 | tf_op jit(solution)/shard_map/ppermute | solution.py:25
  117.6 2.4 %collective-permute-start.4 = (f32[3,2,1]{2,1,0:T(2,128)S(1)}, f32[3,2,1]{2,1,0:T(2,128)S(1)}, u32[]{:S(2)}, u32[]{:S(2)}) collective-permute-start(f32[3,2,1]{2,1,0:T(2,128)S(1)} %get-tuple-element.60), channel_id=1, source_target_pairs={{0,4},{4,8},{8,12},{12,16},{16,20},{20,24},{24,28},{1,5},{5,9},{9,... | collective-permute-start | bytes 80 | tf_op jit(solution)/shard_map/ppermute | solution.py:24
  120.0 3.4 %collective-permute-done.4 = f32[3,2,1]{2,1,0:T(2,128)S(1)} collective-permute-done((f32[3,2,1]{2,1,0:T(2,128)S(1)}, f32[3,2,1]{2,1,0:T(2,128)S(1)}, u32[]{:S(2)}, u32[]{:S(2)}) %collective-permute-start.4) | collective-permute-done | bytes 56 | tf_op jit(solution)/shard_map/ppermute | solution.py:24
  124.8 5.0 %collective-permute-start.7 = (f32[3,1,6]{2,1,0:T(1,128)S(1)}, f32[3,1,6]{2,1,0:T(1,128)S(1)}, u32[]{:S(2)}, u32[]{:S(2)}) collective-permute-start(f32[3,1,6]{2,1,0:T(1,128)S(1)} %get-tuple-element.59), channel_id=1, source_target_pairs={{0,1},{1,2},{2,3},{4,5},{5,6},{6,7},{8,9},{9,10},{10,11},{12,13},{... | collective-permute-start | bytes 224 | tf_op jit(solution)/shard_map/ppermute | solution.py:24
  131.5 1.9 %collective-permute-start.9 = (f32[3,2,1]{2,1,0:T(2,128)S(1)}, f32[3,2,1]{2,1,0:T(2,128)S(1)}, u32[]{:S(2)}, u32[]{:S(2)}) collective-permute-start(f32[3,2,1]{2,1,0:T(2,128)S(1)} %get-tuple-element.57), channel_id=1, source_target_pairs={{4,0},{8,4},{12,8},{16,12},{20,16},{24,20},{28,24},{5,1},{9,5},{13... | collective-permute-start | bytes 80 | tf_op jit(solution)/shard_map/ppermute | solution.py:25
  133.4 2.4 %collective-permute-start.8 = (f32[3,2,1]{2,1,0:T(2,128)S(1)}, f32[3,2,1]{2,1,0:T(2,128)S(1)}, u32[]{:S(2)}, u32[]{:S(2)}) collective-permute-start(f32[3,2,1]{2,1,0:T(2,128)S(1)} %get-tuple-element.56), channel_id=1, source_target_pairs={{0,4},{4,8},{8,12},{12,16},{16,20},{20,24},{24,28},{1,5},{5,9},{9,... | collective-permute-start | bytes 80 | tf_op jit(solution)/shard_map/ppermute | solution.py:24
  135.8 3.4 %collective-permute-done.8 = f32[3,2,1]{2,1,0:T(2,128)S(1)} collective-permute-done((f32[3,2,1]{2,1,0:T(2,128)S(1)}, f32[3,2,1]{2,1,0:T(2,128)S(1)}, u32[]{:S(2)}, u32[]{:S(2)}) %collective-permute-start.8) | collective-permute-done | bytes 56 | tf_op jit(solution)/shard_map/ppermute | solution.py:24
  140.6 4.8 %collective-permute-start.11 = (f32[3,1,6]{2,1,0:T(1,128)S(1)}, f32[3,1,6]{2,1,0:T(1,128)S(1)}, u32[]{:S(2)}, u32[]{:S(2)}) collective-permute-start(f32[3,1,6]{2,1,0:T(1,128)S(1)} %get-tuple-element.55), channel_id=1, source_target_pairs={{0,1},{1,2},{2,3},{4,5},{5,6},{6,7},{8,9},{9,10},{10,11},{12,13},{... | collective-permute-start | bytes 224 | tf_op jit(solution)/shard_map/ppermute | solution.py:24
  147.0 1.9 %collective-permute-start.13 = (f32[3,2,1]{2,1,0:T(2,128)S(1)}, f32[3,2,1]{2,1,0:T(2,128)S(1)}, u32[]{:S(2)}, u32[]{:S(2)}) collective-permute-start(f32[3,2,1]{2,1,0:T(2,128)S(1)} %get-tuple-element.53), channel_id=1, source_target_pairs={{4,0},{8,4},{12,8},{16,12},{20,16},{24,20},{28,24},{5,1},{9,5},{13... | collective-permute-start | bytes 80 | tf_op jit(solution)/shard_map/ppermute | solution.py:25
  149.0 2.4 %collective-permute-start.12 = (f32[3,2,1]{2,1,0:T(2,128)S(1)}, f32[3,2,1]{2,1,0:T(2,128)S(1)}, u32[]{:S(2)}, u32[]{:S(2)}) collective-permute-start(f32[3,2,1]{2,1,0:T(2,128)S(1)} %get-tuple-element.52), channel_id=1, source_target_pairs={{0,4},{4,8},{8,12},{12,16},{16,20},{20,24},{24,28},{1,5},{5,9},{9,... | collective-permute-start | bytes 80 | tf_op jit(solution)/shard_map/ppermute | solution.py:24
  151.4 3.4 %collective-permute-done.12 = f32[3,2,1]{2,1,0:T(2,128)S(1)} collective-permute-done((f32[3,2,1]{2,1,0:T(2,128)S(1)}, f32[3,2,1]{2,1,0:T(2,128)S(1)}, u32[]{:S(2)}, u32[]{:S(2)}) %collective-permute-start.12) | collective-permute-done | bytes 56 | tf_op jit(solution)/shard_map/ppermute | solution.py:24
  156.2 4.8 %collective-permute-start.15 = (f32[3,1,6]{2,1,0:T(1,128)S(1)}, f32[3,1,6]{2,1,0:T(1,128)S(1)}, u32[]{:S(2)}, u32[]{:S(2)}) collective-permute-start(f32[3,1,6]{2,1,0:T(1,128)S(1)} %get-tuple-element.51), channel_id=1, source_target_pairs={{0,1},{1,2},{2,3},{4,5},{5,6},{6,7},{8,9},{9,10},{10,11},{12,13},{... | collective-permute-start | bytes 224 | tf_op jit(solution)/shard_map/ppermute | solution.py:24
  (84 shorter events, 20.1 us)
Async XLA Ops:
  5.1 8.2 %copy-start.3 = (s32[3,2,4]{2,1,0:T(2,128)S(1)}, s32[3,2,4]{2,1,0:T(2,128)}, u32[]{:S(2)}) copy-start(s32[3,2,4]{2,1,0:T(2,128)} %param.8) | copy-start | bytes 292
  5.1 9.1 %copy-start.5 = (s32[2,4]{1,0:T(2,128)S(1)}, s32[2,4]{1,0:T(2,128)}, u32[]{:S(2)}) copy-start(s32[2,4]{1,0:T(2,128)} %param.9) | copy-start | bytes 100
  5.1 9.3 %copy-start.6 = (f32[33]{0:T(128)S(1)}, f32[33]{0:T(128)}, u32[]{:S(2)}) copy-start(f32[33]{0:T(128)} %constant.42.clone) | copy-start | bytes 400
  7.1 11.3 %collective-permute-start.1 = (bf16[2,64,64,16]{2,3,1,0:T(8,128)(2,1)S(1)}, bf16[2,64,64,16]{2,3,1,0:T(8,128)(2,1)S(1)}, u32[]{:S(2)}, u32[]{:S(2)}) collective-permute-start(bf16[2,64,64,16]{2,3,1,0:T(8,128)(2,1)S(1)} %copy.99), channel_id=1, source_target_pairs={{4,0},{8,4},{12,8},{16,12},{20,16},{24,20},{28,24},{5,1},{9,5},{13... | collective-permute-start | bytes 786440 | tf_op jit(solution)/shard_map/ppermute | solution.py:25
  11.4 11.9 %collective-permute-start = (bf16[2,64,64,16]{2,3,1,0:T(8,128)(2,1)}, bf16[2,64,64,16]{2,3,1,0:T(8,128)(2,1)}, u32[]{:S(2)}, u32[]{:S(2)}) collective-permute-start(bf16[2,64,64,16]{2,3,1,0:T(8,128)(2,1)} %copy.98), channel_id=1, source_target_pairs={{0,4},{4,8},{8,12},{12,16},{16,20},{20,24},{24,28},{1,5},{5,9},{9,... | collective-permute-start | bytes 786440 | tf_op jit(solution)/shard_map/ppermute | solution.py:24
  17.9 8.1 %copy-start = (bf16[2,64,64,128]{3,2,1,0:T(8,128)(2,1)S(1)}, bf16[2,64,64,128]{3,2,1,0:T(8,128)(2,1)}, u32[]{:S(2)}) copy-start(bf16[2,64,64,128]{3,2,1,0:T(8,128)(2,1)} %param.7) | copy-start | bytes 6291460
  25.9 30.1 %copy-start.1 = (bf16[2,64,64,16]{3,2,1,0:T(8,128)(2,1)S(1)}, bf16[2,64,64,16]{3,2,1,0:T(8,128)(2,1)}, u32[]{:S(2)}) copy-start(bf16[2,64,64,16]{3,2,1,0:T(8,128)(2,1)} %copy.65) | copy-start | bytes 786436
  25.9 30.1 %copy-start.2 = (bf16[2,64,64,16]{3,2,1,0:T(8,128)(2,1)S(1)}, bf16[2,64,64,16]{3,2,1,0:T(8,128)(2,1)}, u32[]{:S(2)}) copy-start(bf16[2,64,64,16]{3,2,1,0:T(8,128)(2,1)} %copy.64) | copy-start | bytes 786436
  28.8 26.0 %collective-permute-start.3 = (bf16[2,64,16,160]{3,2,1,0:T(8,128)(2,1)S(1)}, bf16[2,64,16,160]{3,2,1,0:T(8,128)(2,1)S(1)}, u32[]{:S(2)}, u32[]{:S(2)}) collective-permute-start(bf16[2,64,16,160]{3,2,1,0:T(8,128)(2,1)S(1)} %get-tuple-element.29), channel_id=1, source_target_pairs={{1,0},{2,1},{3,2},{5,4},{6,5},{7,6},{9,8},{10,9},{11,10},{13,12},{... | collective-permute-start | bytes 1966088 | tf_op jit(solution)/shard_map/ppermute | solution.py:25
  30.1 25.9 %collective-permute-start.2 = (bf16[2,64,16,160]{3,2,1,0:T(8,128)(2,1)S(1)}, bf16[2,64,16,160]{3,2,1,0:T(8,128)(2,1)S(1)}, u32[]{:S(2)}, u32[]{:S(2)}) collective-permute-start(bf16[2,64,16,160]{3,2,1,0:T(8,128)(2,1)S(1)} %get-tuple-element.28), channel_id=1, source_target_pairs={{0,1},{1,2},{2,3},{4,5},{5,6},{6,7},{8,9},{9,10},{10,11},{12,13},{... | collective-permute-start | bytes 1966088 | tf_op jit(solution)/shard_map/ppermute | solution.py:24
  115.3 47.8 %copy-start.4 = (f32[2,4]{1,0:T(2,128)}, f32[2,4]{1,0:T(2,128)S(1)}, u32[]{:S(2)}) copy-start(f32[2,4]{1,0:T(2,128)S(1)} %get-tuple-element.2) | copy-start | bytes 100
  115.6 4.3 %collective-permute-start.5 = (f32[3,2,1]{2,1,0:T(2,128)S(1)}, f32[3,2,1]{2,1,0:T(2,128)S(1)}, u32[]{:S(2)}, u32[]{:S(2)}) collective-permute-start(f32[3,2,1]{2,1,0:T(2,128)S(1)} %get-tuple-element.61), channel_id=1, source_target_pairs={{4,0},{8,4},{12,8},{16,12},{20,16},{24,20},{28,24},{5,1},{9,5},{13... | collective-permute-start | bytes 80 | tf_op jit(solution)/shard_map/ppermute | solution.py:25
  117.6 5.8 %collective-permute-start.4 = (f32[3,2,1]{2,1,0:T(2,128)S(1)}, f32[3,2,1]{2,1,0:T(2,128)S(1)}, u32[]{:S(2)}, u32[]{:S(2)}) collective-permute-start(f32[3,2,1]{2,1,0:T(2,128)S(1)} %get-tuple-element.60), channel_id=1, source_target_pairs={{0,4},{4,8},{8,12},{12,16},{16,20},{20,24},{24,28},{1,5},{5,9},{9,... | collective-permute-start | bytes 80 | tf_op jit(solution)/shard_map/ppermute | solution.py:24
  123.5 6.4 %collective-permute-start.6 = (f32[3,1,6]{2,1,0:T(1,128)S(1)}, f32[3,1,6]{2,1,0:T(1,128)S(1)}, u32[]{:S(2)}, u32[]{:S(2)}) collective-permute-start(f32[3,1,6]{2,1,0:T(1,128)S(1)} %get-tuple-element.58), channel_id=1, source_target_pairs={{1,0},{2,1},{3,2},{5,4},{6,5},{7,6},{9,8},{10,9},{11,10},{13,12},{... | collective-permute-start | bytes 224 | tf_op jit(solution)/shard_map/ppermute | solution.py:25
  124.8 6.3 %collective-permute-start.7 = (f32[3,1,6]{2,1,0:T(1,128)S(1)}, f32[3,1,6]{2,1,0:T(1,128)S(1)}, u32[]{:S(2)}, u32[]{:S(2)}) collective-permute-start(f32[3,1,6]{2,1,0:T(1,128)S(1)} %get-tuple-element.59), channel_id=1, source_target_pairs={{0,1},{1,2},{2,3},{4,5},{5,6},{6,7},{8,9},{9,10},{10,11},{12,13},{... | collective-permute-start | bytes 224 | tf_op jit(solution)/shard_map/ppermute | solution.py:24
  131.5 4.3 %collective-permute-start.9 = (f32[3,2,1]{2,1,0:T(2,128)S(1)}, f32[3,2,1]{2,1,0:T(2,128)S(1)}, u32[]{:S(2)}, u32[]{:S(2)}) collective-permute-start(f32[3,2,1]{2,1,0:T(2,128)S(1)} %get-tuple-element.57), channel_id=1, source_target_pairs={{4,0},{8,4},{12,8},{16,12},{20,16},{24,20},{28,24},{5,1},{9,5},{13... | collective-permute-start | bytes 80 | tf_op jit(solution)/shard_map/ppermute | solution.py:25
  133.4 5.8 %collective-permute-start.8 = (f32[3,2,1]{2,1,0:T(2,128)S(1)}, f32[3,2,1]{2,1,0:T(2,128)S(1)}, u32[]{:S(2)}, u32[]{:S(2)}) collective-permute-start(f32[3,2,1]{2,1,0:T(2,128)S(1)} %get-tuple-element.56), channel_id=1, source_target_pairs={{0,4},{4,8},{8,12},{12,16},{16,20},{20,24},{24,28},{1,5},{5,9},{9,... | collective-permute-start | bytes 80 | tf_op jit(solution)/shard_map/ppermute | solution.py:24
  139.3 6.2 %collective-permute-start.10 = (f32[3,1,6]{2,1,0:T(1,128)S(1)}, f32[3,1,6]{2,1,0:T(1,128)S(1)}, u32[]{:S(2)}, u32[]{:S(2)}) collective-permute-start(f32[3,1,6]{2,1,0:T(1,128)S(1)} %get-tuple-element.54), channel_id=1, source_target_pairs={{1,0},{2,1},{3,2},{5,4},{6,5},{7,6},{9,8},{10,9},{11,10},{13,12},{... | collective-permute-start | bytes 224 | tf_op jit(solution)/shard_map/ppermute | solution.py:25
  140.6 6.1 %collective-permute-start.11 = (f32[3,1,6]{2,1,0:T(1,128)S(1)}, f32[3,1,6]{2,1,0:T(1,128)S(1)}, u32[]{:S(2)}, u32[]{:S(2)}) collective-permute-start(f32[3,1,6]{2,1,0:T(1,128)S(1)} %get-tuple-element.55), channel_id=1, source_target_pairs={{0,1},{1,2},{2,3},{4,5},{5,6},{6,7},{8,9},{9,10},{10,11},{12,13},{... | collective-permute-start | bytes 224 | tf_op jit(solution)/shard_map/ppermute | solution.py:24
  147.0 4.3 %collective-permute-start.13 = (f32[3,2,1]{2,1,0:T(2,128)S(1)}, f32[3,2,1]{2,1,0:T(2,128)S(1)}, u32[]{:S(2)}, u32[]{:S(2)}) collective-permute-start(f32[3,2,1]{2,1,0:T(2,128)S(1)} %get-tuple-element.53), channel_id=1, source_target_pairs={{4,0},{8,4},{12,8},{16,12},{20,16},{24,20},{28,24},{5,1},{9,5},{13... | collective-permute-start | bytes 80 | tf_op jit(solution)/shard_map/ppermute | solution.py:25
  149.0 5.8 %collective-permute-start.12 = (f32[3,2,1]{2,1,0:T(2,128)S(1)}, f32[3,2,1]{2,1,0:T(2,128)S(1)}, u32[]{:S(2)}, u32[]{:S(2)}) collective-permute-start(f32[3,2,1]{2,1,0:T(2,128)S(1)} %get-tuple-element.52), channel_id=1, source_target_pairs={{0,4},{4,8},{8,12},{12,16},{16,20},{20,24},{24,28},{1,5},{5,9},{9,... | collective-permute-start | bytes 80 | tf_op jit(solution)/shard_map/ppermute | solution.py:24
  154.9 6.2 %collective-permute-start.14 = (f32[3,1,6]{2,1,0:T(1,128)S(1)}, f32[3,1,6]{2,1,0:T(1,128)S(1)}, u32[]{:S(2)}, u32[]{:S(2)}) collective-permute-start(f32[3,1,6]{2,1,0:T(1,128)S(1)} %get-tuple-element.50), channel_id=1, source_target_pairs={{1,0},{2,1},{3,2},{5,4},{6,5},{7,6},{9,8},{10,9},{11,10},{13,12},{... | collective-permute-start | bytes 224 | tf_op jit(solution)/shard_map/ppermute | solution.py:25
  156.2 6.1 %collective-permute-start.15 = (f32[3,1,6]{2,1,0:T(1,128)S(1)}, f32[3,1,6]{2,1,0:T(1,128)S(1)}, u32[]{:S(2)}, u32[]{:S(2)}) collective-permute-start(f32[3,1,6]{2,1,0:T(1,128)S(1)} %get-tuple-element.51), channel_id=1, source_target_pairs={{0,1},{1,2},{2,3},{4,5},{5,6},{6,7},{8,9},{9,10},{10,11},{12,13},{... | collective-permute-start | bytes 224 | tf_op jit(solution)/shard_map/ppermute | solution.py:24

commit v2 on v1

--- a/solution.py
+++ b/solution.py
@@ -14,17 +14,10 @@
 ZSTEP = 4
 
 
-def padded_2(array, sides, width):
-    for axis, dim in sides:
-        devices, length = (lax.axis_size(axis), array.shape[dim])
-        up = [(i, (i + 1) % devices) for i in range(devices - 1)]
-        down = [(j, i) for i, j in up]
-        last = lax.slice_in_dim(array, length - width, length, axis=dim)
-        initial = lax.slice_in_dim(array, 0, width, axis=dim)
-        before = lax.ppermute(last, axis, up)
-        after = lax.ppermute(initial, axis, down)
-        array = jnp.concatenate([before, array, after], axis=dim)
-    return array
+PARTS = 4
+GROUP = 8
+PITCH = 136
+SIDES = [(dx, dy) for dy in (-1, 0, 1) for dx in (-1, 0, 1) if (dx, dy) != (0, 0)]
 
 
 def tables(length, grid_x, grid_y):
@@ -54,18 +47,162 @@
         along_y[1, rows, 0, window] = -sine[:half]
         along_y[1, rows, 1, window] = cosine[:half]
     along_z = np.block([[cosine, sine], [-sine, cosine]])
+    margin = stride // 2
+    own = width - 2 * margin
+    along_x = along_x.reshape(width, 2 * grid_x * length)
+    order = np.zeros((2 * own, along_x.shape[1]), ml_dtypes.bfloat16)
+    order[:own] = along_x[margin : margin + own]
+    order[own : own + margin] = along_x[:margin]
+    order[own + margin : own + 2 * margin] = along_x[margin + own :]
     return (
-        along_x.reshape(width, 2 * grid_x * length),
+        order,
         along_y.reshape(2 * padded, 2 * height),
         along_z,
     )
 
 
+def strip_tables(margin, own):
+    pack = np.zeros((GROUP, own, 2, GROUP, margin), ml_dtypes.bfloat16)
+    unpack = np.zeros((2, GROUP, margin, GROUP, own), ml_dtypes.bfloat16)
+    for g in range(GROUP):
+        for m in range(margin):
+            pack[g, m, 0, g, m] = 1
+            pack[g, own - margin + m, 1, g, m] = 1
+            unpack[0, g, m, g, m] = 1
+            unpack[1, g, m, g, margin + m] = 1
+    return (
+        pack.reshape(GROUP * own, 2 * GROUP * margin),
+        unpack.reshape(2 * GROUP * margin, GROUP * own),
+    )
+
+
+def inside(dx, dy):
+    x = lax.axis_index("gx") + dx
+    y = lax.axis_index("gy") + dy
+    return (x >= 0) & (x < lax.axis_size("gx")) & (y >= 0) & (y < lax.axis_size("gy"))
+
+
+def greet(sides):
+    barrier = pltpu.get_barrier_semaphore()
+    for dx, dy in sides:
+
+        @pl.when(inside(dx, dy))
+        def _():
+            pl.semaphore_signal(
+                barrier,
+                inc=1,
+                device_id={"gx": lax.axis_index("gx") + dx, "gy": lax.axis_index("gy") + dy},
+                device_id_type=pl.DeviceIdType.MESH,
+            )
+
+    pl.semaphore_wait(barrier, sum(inside(dx, dy).astype(jnp.int32) for dx, dy in sides))
+
+
 def spectrum_kernel(
-    grid_x, grid_y, vol, table_x, table_y, table_z, table_e, cos_y, sin_y, out, first, second
+    grid_x,
+    grid_y,
+    vol,
+    pack,
+    unpack,
+    table_x,
+    table_y,
+    table_z,
+    table_e,
+    cos_y,
+    sin_y,
+    out,
+    first,
+    second,
+    strip,
+    side_y,
+    side_x,
+    margins,
+    send_sem,
+    recv_sem,
 ):
     length = vol.shape[1]
-    height = vol.shape[2]
+    tall = vol.shape[2]
+    own = vol.shape[3]
+    margin = length // 4
+    height = tall + 2 * margin
+    depth = length // PARTS
+    chunks = depth // GROUP
+
+    def copy(dx, dy, part):
+        rows = {-1: pl.ds(0, margin), 0: pl.ds(0, tall), 1: pl.ds(tall - margin, margin)}[dy]
+        if dx == 0:
+            zs = pl.ds(part * depth, depth)
+            src = vol.at[:, zs, rows, :]
+            dst = side_y.at[(1 - dy) // 2, :, zs, :, :]
+        else:
+            cs = pl.ds(part * chunks, chunks)
+            to = {
+                1: pl.ds(0, margin),
+                0: pl.ds(margin, tall),
+                -1: pl.ds(tall + margin, margin),
+            }[dy]
+            src = strip.at[(1 + dx) // 2, cs, :, rows, :]
+            dst = side_x.at[(1 - dx) // 2, cs, :, to, :]
+        n = SIDES.index((dx, dy))
+        return pltpu.make_async_remote_copy(
+            src_ref=src,
+            dst_ref=dst,
+            send_sem=send_sem.at[n, part],
+            recv_sem=recv_sem.at[n, part],
+            device_id={"gx": lax.axis_index("gx") + dx, "gy": lax.axis_index("gy") + dy},
+            device_id_type=pl.DeviceIdType.MESH,
+        )
+
+    for side, (dx, dy) in enumerate(((0, -1), (0, 1))):
+
+        @pl.when(jnp.logical_not(inside(dx, dy)))
+        def _():
+            side_y[side] = jnp.zeros(side_y.shape[1:], side_y.dtype)
+
+    for side, dx in enumerate((-1, 1)):
+        for dy, lo, count in ((-1, 0, margin), (0, margin, tall), (1, margin + tall, margin)):
+
+            @pl.when(jnp.logical_not(inside(dx, dy)))
+            def _():
+                side_x[side, :, :, lo : lo + count, :] = jnp.zeros(
+                    (side_x.shape[1], 2, count, side_x.shape[4]), side_x.dtype
+                )
+
+    greet(SIDES)
+
+    def send_rows(part, carry):
+        for dx, dy in SIDES:
+            if dx == 0:
+
+                @pl.when(inside(dx, dy))
+                def _():
+                    copy(dx, dy, part).start()
+
+        return carry
+
+    lax.fori_loop(0, PARTS, send_rows, 0)
+
+    def send_strips(part, carry):
+        for i in range(chunks):
+            c = part * chunks + i
+            wide = jnp.concatenate(
+                [vol[:, c * GROUP + g].reshape(2 * tall, own) for g in range(GROUP)], axis=1
+            )
+            packed = jnp.dot(wide, pack[...], preferred_element_type=jnp.float32)
+            packed = packed.astype(jnp.bfloat16).reshape(2, tall, 2 * GROUP * margin)
+            strip[0, c] = packed[:, :, : GROUP * margin]
+            strip[1, c] = packed[:, :, GROUP * margin :]
+        for dx, dy in SIDES:
+            if dx != 0:
+
+                @pl.when(inside(dx, dy))
+                def _():
+                    copy(dx, dy, part).start()
+
+        return carry
+
+    lax.fori_loop(0, PARTS, send_strips, 0)
+
     half = length // 2 + 1
     lanes = grid_x * length
     padded = table_y.shape[0] // 2
@@ -74,7 +211,10 @@
     def slab(step, carry):
         z0 = step * ZSTEP
         for v in range(2):
-            rows = vol[v, pl.ds(z0, ZSTEP)].reshape(ZSTEP * height, vol.shape[3])
+            zs = pl.ds(z0, ZSTEP)
+            rows = jnp.concatenate([side_y[0, v, zs], vol[v, zs], side_y[1, v, zs]], axis=1)
+            rows = jnp.concatenate([rows, margins[v, zs]], axis=2)
+            rows = rows.reshape(ZSTEP * height, 2 * own)
             one = jnp.dot(rows, table_x[...], preferred_element_type=jnp.float32)
             first[v] = one.astype(jnp.bfloat16)
         for i in range(ZSTEP):
@@ -89,19 +229,38 @@
             two = jnp.dot(table_y[...], right, preferred_element_type=jnp.float32)
             for c in range(2):
                 for t in range(pieces):
-                    second[t, pl.ds(c * length + z0 + i, padded, stride=2 * length), :] = two[
+                    second[t, pl.ds(c * length + z0 + i, padded, stride=PITCH), :] = two[
                         c * padded : (c + 1) * padded, t * 128 : (t + 1) * 128
                     ]
         return carry
 
-    lax.fori_loop(0, length // ZSTEP, slab, 0)
+    def take(part, carry):
+        for dx, dy in SIDES:
+
+            @pl.when(inside(-dx, -dy))
+            def _():
+                copy(dx, dy, part).wait_recv()
+
+        for i in range(chunks):
+            c = part * chunks + i
+            wide = jnp.concatenate(
+                [side_x[s, c].reshape(2 * height, GROUP * margin) for s in range(2)], axis=1
+            )
+            apart = jnp.dot(wide, unpack[...], preferred_element_type=jnp.float32)
+            apart = apart.astype(jnp.bfloat16).reshape(2, height, GROUP * own)
+            for g in range(GROUP):
+                margins[:, c * GROUP + g] = apart[:, :, g * own : (g + 1) * own]
+        steps = depth // ZSTEP
+        return lax.fori_loop(part * steps, (part + 1) * steps, slab, carry)
+
+    lax.fori_loop(0, PARTS, take, 0)
 
     group = lax.broadcasted_iota(jnp.int32, (8, lanes), 1) // length
 
     for j in range(grid_y):
 
         def line(ky, sums):
-            base = pl.multiple_of((j * half + ky) * 2 * length, 2 * length)
+            base = pl.multiple_of((j * half + ky) * PITCH, 8)
             right = jnp.concatenate(
                 [second[t, pl.ds(base, 2 * length), :].astype(jnp.bfloat16) for t in range(pieces)],
                 axis=1,
@@ -129,6 +288,125 @@
         for n in range(6):
             out[j, n] = sums[n]
 
+    def sent(part, carry):
+        for dx, dy in SIDES:
+
+            @pl.when(inside(dx, dy))
+            def _():
+                copy(dx, dy, part).wait_send()
+
+        return carry
+
+    lax.fori_loop(0, PARTS, sent, 0)
+
+
+def reach_of(grid_x, grid_y):
+    far_x, far_y = -(-SWEEPS // grid_x), -(-SWEEPS // grid_y)
+    return far_x, far_y
+
+
+def partners(grid_x, grid_y):
+    far_x, far_y = reach_of(grid_x, grid_y)
+    return [
+        (dx, dy)
+        for dy in range(-far_y, far_y + 1)
+        for dx in range(-far_x, far_x + 1)
+        if (dx, dy) != (0, 0)
+    ]
+
+
+def sweep_kernel(grid_x, grid_y, spacing, mine, out, inbox, grid, send_sem, recv_sem):
+    sides = partners(grid_x, grid_y)
+    far_x, far_y = reach_of(grid_x, grid_y)
+    tall, wide = grid.shape[1:]
+
+    def copy(n):
+        dx, dy = sides[n]
+        return pltpu.make_async_remote_copy(
+            src_ref=mine,
+            dst_ref=inbox.at[n],
+            send_sem=send_sem.at[n],
+            recv_sem=recv_sem.at[n],
+            device_id={"gx": lax.axis_index("gx") + dx, "gy": lax.axis_index("gy") + dy},
+            device_id_type=pl.DeviceIdType.MESH,
+        )
+
+    for n, (dx, dy) in enumerate(sides):
+
+        @pl.when(jnp.logical_not(inside(-dx, -dy)))
+        def _():
+            inbox[n] = jnp.zeros(inbox.shape[1:], inbox.dtype)
+
+    grid[...] = jnp.zeros(grid.shape, grid.dtype)
+    greet(sides)
+    for n, (dx, dy) in enumerate(sides):
+
+        @pl.when(inside(dx, dy))
+        def _():
+            copy(n).start()
+
+    for n, (dx, dy) in enumerate(sides):
+
+        @pl.when(inside(-dx, -dy))
+        def _():
+            copy(n).wait_recv()
+
+    for dy in range(-far_y, far_y + 1):
+        row = None
+        for dx in range(-far_x, far_x + 1):
+            tile = mine[...] if (dx, dy) == (0, 0) else inbox[sides.index((-dx, -dy))]
+            shift = (dx + far_x) * grid_x
+            tile = pltpu.roll(tile, shift, 1) if shift else tile
+            row = tile if row is None else row + tile
+        top = (dy + far_y) * grid_y
+        for c in range(4):
+            grid[c, top : top + grid_y, :] = row[c * grid_y : (c + 1) * grid_y]
+
+    y = lax.broadcasted_iota(jnp.int32, (tall, wide), 0)
+    x = lax.broadcasted_iota(jnp.int32, (tall, wide), 1)
+    y = y + (lax.axis_index("gy") - far_y) * grid_y
+    x = x + (lax.axis_index("gx") - far_x) * grid_x
+    within = (
+        (y >= 0)
+        & (y < lax.axis_size("gy") * grid_y)
+        & (x >= 0)
+        & (x < lax.axis_size("gx") * grid_x)
+    )
+    data = [grid[c] for c in range(3)]
+    mask = grid[3]
+    u = [mask * d for d in data]
+    for _ in range(SWEEPS):
+        east = [pltpu.roll(a, wide - 1, 1) for a in u]
+        west = [pltpu.roll(a, 1, 1) for a in u]
+        north = [pltpu.roll(a, tall - 1, 0) for a in u]
+        south = [pltpu.roll(a, 1, 0) for a in u]
+        ahead = [n - s for n, s in zip(north, south)]
+        cross = [pltpu.roll(a, wide - 1, 1) - pltpu.roll(a, 1, 1) for a in ahead]
+        x_xi = spacing + 0.5 * (east[0] - west[0])
+        y_xi = 0.5 * (east[1] - west[1])
+        x_eta = 0.5 * ahead[0]
+        y_eta = spacing + 0.5 * ahead[1]
+        alpha = x_eta * x_eta + y_eta * y_eta
+        beta = x_xi * x_eta + y_xi * y_eta
+        gamma = x_xi * x_xi + y_xi * y_xi
+        new = []
+        for c in range(3):
+            smooth = (
+                alpha * (east[c] + west[c]) + gamma * (north[c] + south[c]) - 0.5 * beta * cross[c]
+            ) / (2.0 * (alpha + gamma))
+            moved = smooth + 0.5 * mask * (data[c] - smooth)
+            new.append(jnp.where(within, moved, 0.0))
+        u = new
+    top, left = far_y * grid_y, far_x * grid_x
+    for c in range(3):
+        out[c] = pltpu.roll(u[c], wide - left, 1)[top : top + grid_y, :grid_x]
+
+    for n, (dx, dy) in enumerate(sides):
+
+        @pl.when(inside(dx, dy))
+        def _():
+            copy(n).wait_send()
+
 
 def phases(offset, length):
     counter = jnp.arange(length, dtype=jnp.int32)
@@ -136,30 +414,6 @@
     product = jnp.mod(shifts[..., None] * counter, length)
     angle = product.astype(jnp.float32) * (2.0 * math.pi / length)
     return (jnp.cos(angle).astype(jnp.bfloat16), jnp.sin(angle).astype(jnp.bfloat16))
-
-
-def relax(padded, data, mask, spacing):
-    east = padded[:, 1:-1, 2:]
-    west = padded[:, 1:-1, :-2]
-    north = padded[:, 2:, 1:-1]
-    south = padded[:, :-2, 1:-1]
-    north_east = padded[:, 2:, 2:]
-    north_west = padded[:, 2:, :-2]
-    south_east = padded[:, :-2, 2:]
-    south_west = padded[:, :-2, :-2]
-    x_xi = spacing + 0.5 * (east[0] - west[0])
-    y_xi = 0.5 * (east[1] - west[1])
-    x_eta = 0.5 * (north[0] - south[0])
-    y_eta = spacing + 0.5 * (north[1] - south[1])
-    alpha = x_eta * x_eta + y_eta * y_eta
-    beta = x_xi * x_eta + y_xi * y_eta
-    gamma = x_xi * x_xi + y_xi * y_xi
-    smooth = (
-        alpha * (east + west)
-        + gamma * (north + south)
-        - 0.5 * beta * (north_east - north_west - south_east + south_west)
-    ) / (2.0 * (alpha + gamma))
-    return smooth + 0.5 * mask * (data - smooth)
 
 
 def body(volumes, peaks, valid):
@@ -169,7 +423,8 @@
     half = length // 2 + 1
     _, grid_y, grid_x = peaks.shape
     lanes = grid_x * length
-    padded = padded_2(volumes, (("gx", 3), ("gy", 2)), margin)
+    tall, own = volumes.shape[2:]
+    height = tall + 2 * margin
     table_x, table_y, table_z = tables(length, grid_x, grid_y)
     cosine, sine = phases(peaks, length)
     cos_z, sin_z = cosine[2], sine[2]
@@ -192,15 +447,23 @@
     sums = pl.pallas_call(
         functools.partial(spectrum_kernel, grid_x, grid_y),
         out_shape=jax.ShapeDtypeStruct((grid_y, 6, 8, lanes), jnp.float32),
-        in_specs=[pl.BlockSpec(memory_space=pltpu.VMEM)] * 7,
+        in_specs=[pl.BlockSpec(memory_space=pltpu.VMEM)] * 9,
         out_specs=pl.BlockSpec(memory_space=pltpu.VMEM),
         scratch_shapes=[
-            pltpu.VMEM((2, ZSTEP * padded.shape[2], 2 * lanes), jnp.bfloat16),
-            pltpu.VMEM((2 * lanes // 128, table_y.shape[0] * length, 128), jnp.float32),
+            pltpu.VMEM((2, ZSTEP * height, 2 * lanes), jnp.bfloat16),
+            pltpu.VMEM((2 * lanes // 128, table_y.shape[0] // 2 * PITCH, 128), jnp.float32),
+            pltpu.VMEM((2, length // GROUP, 2, tall, GROUP * margin), jnp.bfloat16),
+            pltpu.VMEM((2, 2, length, margin, own), jnp.bfloat16),
+            pltpu.VMEM((2, length // GROUP, 2, height, GROUP * margin), jnp.bfloat16),
+            pltpu.VMEM((2, length, height, own), jnp.bfloat16),
+            pltpu.SemaphoreType.DMA((len(SIDES), PARTS)),
+            pltpu.SemaphoreType.DMA((len(SIDES), PARTS)),
         ],
-        compiler_params=pltpu.CompilerParams(vmem_limit_bytes=56 * 1024 * 1024),
+        compiler_params=pltpu.CompilerParams(
+            vmem_limit_bytes=56 * 1024 * 1024, collective_id=0, has_side_effects=True
+        ),
         name="spectrum",
-    )(padded, table_x, table_y, table_z, table_e, spread(cosine[1]), spread(sine[1]))
+    )(volumes, *strip_tables(margin, own), table_x, table_y, table_z, table_e, spread(cosine[1]), spread(sine[1]))
 
     sums = sums.reshape(grid_y, 3, 2, 8, grid_x, length)
     factor = 1.0 / (length * math.sqrt(length))
@@ -218,10 +481,26 @@
     shift = jnp.tanh((lower - upper) / (jnp.abs(lower + upper - 2.0 * centre) + 0.5))
     data = peaks.astype(jnp.float32) + shift
     mask = valid.astype(jnp.float32)
-    moved = mask * data
-    for _ in range(SWEEPS):
-        rimmed = padded_2(moved, (("gx", 2), ("gy", 1)), 1)
-        moved = relax(rimmed, data, mask, float(stride))
+    far_x, far_y = reach_of(grid_x, grid_y)
+    tall = -(-(2 * far_y + 1) * grid_y // 8) * 8
+    wide = -(-(2 * far_x + 1) * grid_x // 128) * 128
+    mine = jnp.concatenate([data, mask[None]]).reshape(4 * grid_y, grid_x)
+    mine = jnp.pad(mine, ((0, 0), (0, wide - grid_x)))
+    count = len(partners(grid_x, grid_y))
+    moved = pl.pallas_call(
+        functools.partial(sweep_kernel, grid_x, grid_y, float(stride)),
+        out_shape=jax.ShapeDtypeStruct(data.shape, jnp.float32),
+        in_specs=[pl.BlockSpec(memory_space=pltpu.VMEM)],
+        out_specs=pl.BlockSpec(memory_space=pltpu.VMEM),
+        scratch_shapes=[
+            pltpu.VMEM((count, 4 * grid_y, wide), jnp.float32),
+            pltpu.VMEM((4, tall, wide), jnp.float32),
+            pltpu.SemaphoreType.DMA((count,)),
+            pltpu.SemaphoreType.DMA((count,)),
+        ],
+        compiler_params=pltpu.CompilerParams(collective_id=1, has_side_effects=True),
+        name="sweeps",
+    )(mine)
     return (moved, centre)
 
 

time: 165 us -> 74.4 us (0.45)
  starting transfers between devices: 42 us -> 0 us
  waiting for transfers between devices: 38.6 us -> 0 us
  Pallas kernels: 49.5 us -> 63.5 us
  other arithmetic: 14.9 us -> 3.43 us
  local copies, waits for them, and re-layouts: 17.2 us -> 6.38 us
    ppermute x16 -> x0, starting transfers between devices: 42 us -> none  [the longest x8 28.3 us: padded_2(): before = lax.ppermute(last, axis, up)]
    ppermute x16 -> x0, waiting for transfers between devices: 38.6 us -> none  [the longest x8 20.5 us: padded_2(): after = lax.ppermute(initial, axis, down)]
    concatenate x7 -> x1, other arithmetic: 9.18 us -> 0.01 us  [body(): mine = jnp.concatenate([data, mask[None]]).reshape(4 * grid_y, grid_x)]
    pallas_call x0 -> x1, Pallas kernels: none -> 8.23 us  [body(): pl.pallas_call(functools.partial(sweep_kernel, grid_x, grid_y, float(stri...]
    pallas_call x1, Pallas kernels: 49.5 us -> 55.3 us  [body(): pl.pallas_call(functools.partial(spectrum_kernel, grid_x, grid_y), out_sh...]
    slice x7 -> x0, local copies, waits for them, and re-layouts: 4.69 us -> none  [the longest x4 4.67 us: padded_2(): last = lax.slice_in_dim(array, length - width, length, axis=dim)]
    ppermute x2 -> x0, local copies, waits for them, and re-layouts: 4.4 us -> none  [the longest x1 2.64 us: padded_2(): before = lax.ppermute(last, axis, up)]
    slice x1 -> x0, other arithmetic: 2.87 us -> none  [padded_2(): last = lax.slice_in_dim(array, length - width, length, axis=dim)]
  transfers between devices with their start and end apart: 16 -> 0, of which waited for: 10 -> 0; matrix products, arithmetic and copies ran while one was open for 5% -> 0% of each run, Pallas kernels for 0% -> 0%
where the time goes in v2:
time: 74.4 us; the launch traced here: 74.1 us
  Pallas kernels  63.5 us (85%)
  local copies, waits for them, and re-layouts  6.38 us (9%)
  other arithmetic  3.43 us (5%)
  between operations  0.77 us (1%)
    pallas_call x1, Pallas kernels, body(): pl.pallas_call(functools.partial(spectrum_kernel, grid_x, grid_y), out_sh...  55.3 us
    pallas_call x1, Pallas kernels, body(): pl.pallas_call(functools.partial(sweep_kernel, grid_x, grid_y, float(stri...  8.23 us
    reshape x4, local copies, waits for them, and re-layouts, spread(): return table.reshape(grid_y, 3, half, lanes)  2.05 us

profile of v2, /device:TPU:4, one launch (start us, length us, event | category | flops | bytes accessed | tf_op | source)
XLA Modules:
  0.0 74.1 jit_solution(15935524883898561050)
XLA Ops:
  0.6 0.7 convert_bitcast_fusion
  1.3 0.7 add_add_fusion
  2.0 0.2 fusion.48
  2.2 0.2 multiply_bitcast_fusion
  2.4 0.3 fusion.49
  2.7 0.4 cosine_convert_fusion
  3.2 0.6 pad_bitcast_fusion.table_e
  3.8 0.7 multiply_bitcast_fusion.2
  4.4 0.1 copy.38
  4.6 0.1 copy.36
  4.7 0.3 broadcast_in_dim.6
  5.0 0.3 reshape.51
  5.3 0.7 copy.39.cos_y
  6.0 0.3 broadcast_in_dim.7
  6.3 0.3 reshape.52
  6.6 0.7 copy.40.sin_y
  7.3 55.3 %spectrum.1 = f32[2,6,8,256]{3,2,1,0:T(8,128)} custom-call(bf16[2,64,64,128]{3,2,1,0:T(8,128)(2,1)} %vol.1, bf16[1024,256]{1,0:T(8,128)(2,1)} %constant.45.clone.pack, bf16[256,1024]{1,0:T(8,128)(2,1)} %constant.46.clone.unpack, bf16[256,512]{1,0:T(8,128)(2,1)} %constant.47.clone.table_x, bf16[144,192]{1,0:T(8,128)(2,1)} %constant.48.clone.table_y, ...), custom_call_target="tpu_custom_call" | custom-call | tf_op jit(solution)/shard_map/spectrum/pallas_call | solution.py:447
  62.6 1.0 %reshape.53 = f32[2,3,2,8,4,64]{5,4,3,2,1,0:T(4,128)S(1)} reshape(f32[2,6,8,256]{3,2,1,0:T(8,128)} %spectrum.1) | data formatting | bytes 196608 | tf_op jit(solution)/shard_map/reshape | solution.py:468
  63.7 0.1 fusion.36
  63.7 0.1 fusion.42
  63.8 0.1 subtract_reduce_fusion
  64.0 0.6 pad.9.mine
  64.6 8.2 %sweeps.1 = f32[3,2,4]{2,1,0:T(2,128)} custom-call(f32[8,128]{1,0:T(8,128)} %pad.9.mine), custom_call_target="tpu_custom_call" | custom-call | tf_op jit(solution)/shard_map/sweeps/pallas_call | solution.py:490
  72.9 1.3 %copy.101 = f32[3,2,4]{2,1,0:T(2,128)} copy(f32[3,2,4]{2,1,0:T(2,128)} %sweeps.1) | data formatting | bytes 192
  (14 shorter events, 0.2 us)
Async XLA Ops:
  7.3 56.6 %copy-start = (s32[3,2,4]{2,1,0:T(2,128)S(1)}, s32[3,2,4]{2,1,0:T(2,128)}, u32[]{:S(2)}) copy-start(s32[3,2,4]{2,1,0:T(2,128)} %param.10) | copy-start | bytes 292
  63.9 10.2 %copy-start.1 = (f32[2,4]{1,0:T(2,128)}, f32[2,4]{1,0:T(2,128)S(1)}, u32[]{:S(2)}) copy-start(f32[2,4]{1,0:T(2,128)S(1)} %get-tuple-element.19) | copy-start | bytes 100

commit v3 on v1

v3 whole, which is shorter than its diff:
```python
import functools
import math

import jax
import jax.numpy as jnp
import ml_dtypes
import numpy as np
from jax import lax
from jax.experimental import pallas as pl
from jax.experimental.pallas import tpu as pltpu
from jax.sharding import PartitionSpec as P

SWEEPS = 3
ZSTEP = 4
LINES = 3


PARTS = 4
GROUP = 8
PITCH = 136
SIDES = [(dx, dy) for dy in (-1, 0, 1) for dx in (-1, 0, 1) if (dx, dy) != (0, 0)]


def tables(length, grid_x, grid_y):
    counter = np.arange(length)
    angle = (counter[:, None] * counter[None, :] % length).astype(np.float32) * np.float32(
        2.0 * math.pi / length
    )
    factor = np.float32(1.0 / math.sqrt(length))
    cosine = (np.cos(angle) * factor).astype(ml_dtypes.bfloat16)
    sine = (np.sin(angle) * factor).astype(ml_dtypes.bfloat16)
    stride = length // 2
    half = length // 2 + 1
    width = stride * grid_x + stride
    height = stride * grid_y + stride
    along_x = np.zeros((width, 2, grid_x, length), ml_dtypes.bfloat16)
    for i in range(grid_x):
        along_x[i * stride : i * stride + length, 0, i] = cosine
        along_x[i * stride : i * stride + length, 1, i] = -sine
    lines = grid_y * half
    padded = -(-lines // 8) * 8
    along_y = np.zeros((2, padded, 2, height), ml_dtypes.bfloat16)
    for j in range(grid_y):
        rows = slice(j * half, (j + 1) * half)
        window = slice(j * stride, j * stride + length)
        along_y[0, rows, 0, window] = cosine[:half]
        along_y[0, rows, 1, window] = sine[:half]
        along_y[1, rows, 0, window] = -sine[:half]
        along_y[1, rows, 1, window] = cosine[:half]
    along_z = np.block([[cosine, sine], [-sine, cosine]])
    margin = stride // 2
    own = width - 2 * margin
    along_x = along_x.reshape(width, 2 * grid_x * length)
    order = np.zeros((2 * own, along_x.shape[1]), ml_dtypes.bfloat16)
    order[:own] = along_x[margin : margin + own]
    order[own : own + margin] = along_x[:margin]
    order[own + margin : own + 2 * margin] = along_x[margin + own :]
    return (
        order,
        along_y.reshape(2 * padded, 2 * height),
        along_z,
    )


def strip_tables(margin, own):
    pack = np.zeros((GROUP, own, 2, GROUP, margin), ml_dtypes.bfloat16)
    unpack = np.zeros((2, GROUP, margin, GROUP, own), ml_dtypes.bfloat16)
    for g in range(GROUP):
        for m in range(margin):
            pack[g, m, 0, g, m] = 1
            pack[g, own - margin + m, 1, g, m] = 1
            unpack[0, g, m, g, m] = 1
            unpack[1, g, m, g, margin + m] = 1
    return (
        pack.reshape(GROUP * own, 2 * GROUP * margin),
        unpack.reshape(2 * GROUP * margin, GROUP * own),
    )


def inside(dx, dy):
    x = lax.axis_index("gx") + dx
    y = lax.axis_index("gy") + dy
    return (x >= 0) & (x < lax.axis_size("gx")) & (y >= 0) & (y < lax.axis_size("gy"))


def greet(sides):
    barrier = pltpu.get_barrier_semaphore()
    for dx, dy in sides:

        @pl.when(inside(dx, dy))
        def _():
            pl.semaphore_signal(
                barrier,
                inc=1,
                device_id={"gx": lax.axis_index("gx") + dx, "gy": lax.axis_index("gy") + dy},
                device_id_type=pl.DeviceIdType.MESH,
            )

    pl.semaphore_wait(barrier, sum(inside(dx, dy).astype(jnp.int32) for dx, dy in sides))


def reach_of(grid_x, grid_y):
    far_x, far_y = -(-SWEEPS // grid_x), -(-SWEEPS // grid_y)
    return far_x, far_y


def partners(grid_x, grid_y):
    far_x, far_y = reach_of(grid_x, grid_y)
    return [
        (dx, dy)
        for dy in range(-far_y, far_y + 1)
        for dx in range(-far_x, far_x + 1)
        if (dx, dy) != (0, 0)
    ]


def sweep(grid_x, grid_y, spacing, mine, out, inbox, grid, send_sem, recv_sem):
    sides = partners(grid_x, grid_y)
    far_x, far_y = reach_of(grid_x, grid_y)
    tall, wide = grid.shape[1:]

    def copy(n):
        dx, dy = sides[n]
        return pltpu.make_async_remote_copy(
            src_ref=mine,
            dst_ref=inbox.at[n],
            send_sem=send_sem.at[n],
            recv_sem=recv_sem.at[n],
            device_id={"gx": lax.axis_index("gx") + dx, "gy": lax.axis_index("gy") + dy},
            device_id_type=pl.DeviceIdType.MESH,
        )

    for n, (dx, dy) in enumerate(sides):

        @pl.when(inside(dx, dy))
        def _():
            copy(n).start()

    for n, (dx, dy) in enumerate(sides):

        @pl.when(inside(-dx, -dy))
        def _():
            copy(n).wait_recv()

    for dy in range(-far_y, far_y + 1):
        row = None
        for dx in range(-far_x, far_x + 1):
            tile = mine[...] if (dx, dy) == (0, 0) else inbox[sides.index((-dx, -dy))]
            shift = (dx + far_x) * grid_x
            tile = pltpu.roll(tile, shift, 1) if shift else tile
            row = tile if row is None else row + tile
        top = (dy + far_y) * grid_y
        for c in range(4):
            grid[c, top : top + grid_y, :] = row[c * grid_y : (c + 1) * grid_y]

    y = lax.broadcasted_iota(jnp.int32, (tall, wide), 0)
    x = lax.broadcasted_iota(jnp.int32, (tall, wide), 1)
    y = y + (lax.axis_index("gy") - far_y) * grid_y
    x = x + (lax.axis_index("gx") - far_x) * grid_x
    within = (
        (y >= 0)
        & (y < lax.axis_size("gy") * grid_y)
        & (x >= 0)
        & (x < lax.axis_size("gx") * grid_x)
    )
    data = [grid[c] for c in range(3)]
    mask = grid[3]
    u = [mask * d for d in data]
    for _ in range(SWEEPS):
        east = [pltpu.roll(a, wide - 1, 1) for a in u]
        west = [pltpu.roll(a, 1, 1) for a in u]
        north = [pltpu.roll(a, tall - 1, 0) for a in u]
        south = [pltpu.roll(a, 1, 0) for a in u]
        ahead = [n - s for n, s in zip(north, south)]
        cross = [pltpu.roll(a, wide - 1, 1) - pltpu.roll(a, 1, 1) for a in ahead]
        x_xi = spacing + 0.5 * (east[0] - west[0])
        y_xi = 0.5 * (east[1] - west[1])
        x_eta = 0.5 * ahead[0]
        y_eta = spacing + 0.5 * ahead[1]
        alpha = x_eta * x_eta + y_eta * y_eta
        beta = x_xi * x_eta + y_xi * y_eta
        gamma = x_xi * x_xi + y_xi * y_xi
        new = []
        for c in range(3):
            smooth = (
                alpha * (east[c] + west[c]) + gamma * (north[c] + south[c]) - 0.5 * beta * cross[c]
            ) / (2.0 * (alpha + gamma))
            moved = smooth + 0.5 * mask * (data[c] - smooth)
            new.append(jnp.where(within, moved, 0.0))
        u = new
    top, left = far_y * grid_y, far_x * grid_x
    for c in range(3):
        out[c] = pltpu.roll(u[c], wide - left, 1)[top : top + grid_y, :grid_x]

    for n, (dx, dy) in enumerate(sides):

        @pl.when(inside(dx, dy))
        def _():
            copy(n).wait_send()


def clear_inbox(grid_x, grid_y, inbox, grid):
    for n, (dx, dy) in enumerate(partners(grid_x, grid_y)):

        @pl.when(jnp.logical_not(inside(-dx, -dy)))
        def _():
            inbox[n] = jnp.zeros(inbox.shape[1:], inbox.dtype)

    grid[...] = jnp.zeros(grid.shape, grid.dtype)


def turn(count, length):
    def wave(steps):
        y = (jnp.abs(steps - length // 2) - length // 4).astype(jnp.float32)
        y = y * (2.0 * math.pi / length)
        t = y * y
        value = -1.0 / 39916800.0
        for term in (1.0 / 362880.0, -1.0 / 5040.0, 1.0 / 120.0, -1.0 / 6.0, 1.0):
            value = value * t + term
        return (value * y).astype(jnp.bfloat16).astype(jnp.float32)

    whole = length - 1
    return wave(count & whole), wave((count - length // 4) & whole)


def phase_tables(grid_x, grid_y, length, peaks, table_e, cos_y, sin_y):
    half = length // 2 + 1
    lines, lanes = cos_y.shape[2:]
    own = lax.broadcasted_iota(jnp.int32, (lines, lanes), 1) // length
    k = lax.broadcasted_iota(jnp.int32, (lines, lanes), 0)
    weight = jnp.where((k == 0) | (k == half - 1), 1.0, 2.0)
    row = lax.broadcasted_iota(jnp.int32, table_e.shape[1:], 0)
    lane = lax.broadcasted_iota(jnp.int32, table_e.shape[1:], 1)
    outer, inner = row & 1, lane // length
    for j in range(grid_y):
        peak = jnp.zeros((lines, lanes), jnp.int32)
        deep = jnp.zeros(table_e.shape[1:], jnp.int32)
        for i in range(grid_x):
            peak = jnp.where(own == i, peaks[1, j, i], peak)
            deep = jnp.where(row // 8 == i, peaks[2, j, i], deep)
        for o in range(3):
            cosine, sine = turn((peak + (o - 1)) * k, length)
            cos_y[j, o] = cosine * weight
            sin_y[j, o] = sine * weight
        offset = deep + (row & 7) // 2 - 1
        cosine, sine = turn(offset * (lane & (length - 1)), length)
        signed = jnp.where(outer == 0, -sine, sine)
        table_e[j] = jnp.where(outer == inner, cosine, signed).astype(jnp.bfloat16)


def measure_peaks(grid_x, grid_y, length, peaks, valid, sums, group, mine, score):
    lanes = group.shape[1]
    wide = mine.shape[1]
    k = lax.broadcasted_iota(jnp.int32, (8, lanes), 1) & (length - 1)
    o = lax.broadcasted_iota(jnp.int32, (8, lanes), 0)
    column = lax.broadcasted_iota(jnp.int32, (8, wide), 1)
    line = lax.broadcasted_iota(jnp.int32, (8, wide), 0)
    factor = 1.0 / (length * math.sqrt(length))
    for j in range(grid_y):
        peak = jnp.zeros((8, lanes), jnp.int32)
        for i in range(grid_x):
            peak = jnp.where(group == i, peaks[0, j, i], peak)
        cos_x, sin_x = turn((peak + (o - 1)) * k, length)

        def corr(ox, oy, oz):
            by_cos, by_sin = sums[j][2 * oy], sums[j][2 * oy + 1]
            re, im = slice(2 * oz, 2 * oz + 1), slice(2 * oz + 1, 2 * oz + 2)
            real = by_cos[re] - by_sin[im]
            imag = by_sin[re] + by_cos[im]
            return real * cos_x[ox : ox + 1] - imag * sin_x[ox : ox + 1]

        spots = [(1, 1, 1), (0, 1, 1), (1, 0, 1), (1, 1, 0), (2, 1, 1), (1, 2, 1), (1, 1, 2)]
        rows = [corr(*spot) for spot in spots]
        rows = jnp.concatenate(rows + [jnp.zeros_like(rows[0])], axis=0)
        cube = jnp.zeros((8, wide), jnp.float32)
        start = jnp.zeros((8, wide), jnp.float32)
        trust = jnp.zeros((8, wide), jnp.float32)
        for i in range(grid_x):
            total = jnp.sum(jnp.where(group == i, rows, 0.0), axis=1, keepdims=True)
            cube = jnp.where(column == i, total * factor, cube)
            trust = jnp.where(column == i, valid[j, i].astype(jnp.float32), trust)
            for c in range(3):
                here = (column == i) & (line == c)
                start = jnp.where(here, peaks[c, j, i].astype(jnp.float32), start)
        centre = cube[0:1]
        lower, upper = cube[1:4], cube[4:7]
        shift = jnp.tanh((lower - upper) / (jnp.abs(lower + upper - 2.0 * centre) + 0.5))
        data = start[:3] + shift
        for c in range(3):
            mine[c * grid_y + j : c * grid_y + j + 1, :] = data[c : c + 1]
        mine[3 * grid_y + j : 3 * grid_y + j + 1, :] = trust[:1]
        score[j : j + 1, :] = centre[:, :grid_x]


def spectrum_kernel(
    grid_x,
    grid_y,
    vol,
    pack,
    unpack,
    table_x,
    table_y,
    table_z,
    peaks,
    valid,
    moved,
    score,
    table_e,
    cos_y,
    sin_y,
    first,
    second,
    strip,
    side_y,
    side_x,
    margins,
    send_sem,
    recv_sem,
    mine,
    inbox,
    grid,
    sweep_send,
    sweep_recv,
):
    length = vol.shape[1]
    tall = vol.shape[2]
    own = vol.shape[3]
    margin = length // 4
    height = tall + 2 * margin
    depth = length // PARTS
    chunks = depth // GROUP

    def copy(dx, dy, part):
        rows = {-1: pl.ds(0, margin), 0: pl.ds(0, tall), 1: pl.ds(tall - margin, margin)}[dy]
        if dx == 0:
            zs = pl.ds(part * depth, depth)
            src = vol.at[:, zs, rows, :]
            dst = side_y.at[(1 - dy) // 2, :, zs, :, :]
        else:
            cs = pl.ds(part * chunks, chunks)
            to = {
                1: pl.ds(0, margin),
                0: pl.ds(margin, tall),
                -1: pl.ds(tall + margin, margin),
            }[dy]
            src = strip.at[(1 + dx) // 2, cs, :, rows, :]
            dst = side_x.at[(1 - dx) // 2, cs, :, to, :]
        n = SIDES.index((dx, dy))
        return pltpu.make_async_remote_copy(
            src_ref=src,
            dst_ref=dst,
            send_sem=send_sem.at[n, part],
            recv_sem=recv_sem.at[n, part],
            device_id={"gx": lax.axis_index("gx") + dx, "gy": lax.axis_index("gy") + dy},
            device_id_type=pl.DeviceIdType.MESH,
        )

    for side, (dx, dy) in enumerate(((0, -1), (0, 1))):

        @pl.when(jnp.logical_not(inside(dx, dy)))
        def _():
            side_y[side] = jnp.zeros(side_y.shape[1:], side_y.dtype)

    for side, dx in enumerate((-1, 1)):
        for dy, lo, count in ((-1, 0, margin), (0, margin, tall), (1, margin + tall, margin)):

            @pl.when(jnp.logical_not(inside(dx, dy)))
            def _():
                side_x[side, :, :, lo : lo + count, :] = jnp.zeros(
                    (side_x.shape[1], 2, count, side_x.shape[4]), side_x.dtype
                )

    clear_inbox(grid_x, grid_y, inbox, grid)
    greet(partners(grid_x, grid_y))

    def send_strips(part, carry):
        for dx, dy in SIDES:
            if dx == 0:

                @pl.when(inside(dx, dy))
                def _():
                    copy(dx, dy, part).start()

        for i in range(chunks):
            c = part * chunks + i
            wide = jnp.concatenate(
                [vol[:, c * GROUP + g].reshape(2 * tall, own) for g in range(GROUP)], axis=1
            )
            packed = jnp.dot(wide, pack[...], preferred_element_type=jnp.float32)
            packed = packed.astype(jnp.bfloat16).reshape(2, tall, 2 * GROUP * margin)
            strip[0, c] = packed[:, :, : GROUP * margin]
            strip[1, c] = packed[:, :, GROUP * margin :]
        for dx, dy in SIDES:
            if dx != 0:

                @pl.when(inside(dx, dy))
                def _():
                    copy(dx, dy, part).start()

        return carry

    lax.fori_loop(0, PARTS, send_strips, 0)

    half = length // 2 + 1
    lanes = grid_x * length
    padded = table_y.shape[0] // 2
    pieces = 2 * lanes // 128

    group = lax.broadcasted_iota(jnp.int32, (8, lanes), 1) // length
    phase_tables(grid_x, grid_y, length, peaks, table_e, cos_y, sin_y)

    def widen(part, lo, count):
        for i in range(chunks):
            c = part * chunks + i
            wide = jnp.concatenate(
                [
                    side_x[s, c, :, lo : lo + count, :].reshape(2 * count, GROUP * margin)
                    for s in range(2)
                ],
                axis=1,
            )
            apart = jnp.dot(wide, unpack[...], preferred_element_type=jnp.float32)
            apart = apart.astype(jnp.bfloat16).reshape(2, count, GROUP * own)
            for g in range(GROUP):
                margins[:, c * GROUP + g, lo : lo + count, :] = apart[
                    :, :, g * own : (g + 1) * own
                ]

    def along_x(v, zs, rows, lo, count):
        rows = jnp.concatenate([rows, margins[v, zs, lo : lo + count, :]], axis=2)
        rows = rows.reshape(ZSTEP * count, 2 * own)
        one = jnp.dot(rows, table_x[...], preferred_element_type=jnp.float32)
        one = one.astype(jnp.bfloat16).reshape(ZSTEP, count, 2 * lanes)
        first[v, zs, lo : lo + count, :] = one

    steps = depth // ZSTEP

    def take_middle(part, carry):
        for dx, dy in SIDES:
            if dy == 0:

                @pl.when(inside(-dx, -dy))
                def _():
                    copy(dx, dy, part).wait_recv()

        widen(part, margin, tall)

        def middle(step, carry):
            zs = pl.ds(step * ZSTEP, ZSTEP)
            for v in range(2):
                along_x(v, zs, vol[v, zs], margin, tall)
            return carry

        return lax.fori_loop(part * steps, (part + 1) * steps, middle, carry)

    lax.fori_loop(0, PARTS, take_middle, 0)

    def slab(step, carry):
        z0 = step * ZSTEP
        zs = pl.ds(z0, ZSTEP)
        for v in range(2):
            along_x(v, zs, side_y[0, v, zs], 0, margin)
            along_x(v, zs, side_y[1, v, zs], margin + tall, margin)
        for i in range(ZSTEP):
            z = z0 + i
            right = jnp.concatenate(
                [
                    jnp.concatenate([first[0, z, :, :lanes], first[1, z, :, :lanes]], axis=1),
                    jnp.concatenate([first[0, z, :, lanes:], first[1, z, :, lanes:]], axis=1),
                ],
                axis=0,
            )
            two = jnp.dot(table_y[...], right, preferred_element_type=jnp.float32)
            for c in range(2):
                for t in range(pieces):
                    second[t, pl.ds(c * length + z, padded, stride=PITCH), :] = two[
                        c * padded : (c + 1) * padded, t * 128 : (t + 1) * 128
                    ]
        return carry

    def take_ends(part, carry):
        for dx, dy in SIDES:
            if dy != 0:

                @pl.when(inside(-dx, -dy))
                def _():
                    copy(dx, dy, part).wait_recv()

        widen(part, 0, margin)
        widen(part, margin + tall, margin)
        return lax.fori_loop(part * steps, (part + 1) * steps, slab, carry)

    lax.fori_loop(0, PARTS, take_ends, 0)

    def one_line(j, ky, sums):
        base = pl.multiple_of((j * half + ky) * PITCH, 8)
        right = jnp.concatenate(
            [second[t, pl.ds(base, 2 * length), :].astype(jnp.bfloat16) for t in range(pieces)],
            axis=1,
        )
        three = jnp.dot(table_z[...], right, preferred_element_type=jnp.float32)
        re1, im1 = three[:length, :lanes], three[length:, :lanes]
        re2, im2 = three[:length, lanes:], three[length:, lanes:]
        size = (re1 * re1 + im1 * im1) * (re2 * re2 + im2 * im2)
        scale = 1.0 / (jnp.sqrt(size) + 1.0)
        real_r = ((re1 * re2 + im1 * im2) * scale).astype(jnp.bfloat16)
        imag_r = ((im1 * re2 - re1 * im2) * scale).astype(jnp.bfloat16)
        both = jnp.concatenate([real_r, imag_r], axis=0)
        along = jnp.dot(table_e[j], both, preferred_element_type=jnp.float32)
        own_rows = along[:8]
        for i in range(1, grid_x):
            own_rows = jnp.where(group == i, along[8 * i : 8 * i + 8], own_rows)
        new = []
        for o in range(3):
            new.append(sums[2 * o] + own_rows * cos_y[j, o, pl.ds(ky, 1), :])
            new.append(sums[2 * o + 1] + own_rows * sin_y[j, o, pl.ds(ky, 1), :])
        return tuple(new)

    def line(step, sums):
        for i in range(LINES):
            ky = step * LINES + i
            sums = tuple(one_line(j, ky, sums[j]) for j in range(grid_y))
        return sums

    zero = jnp.zeros((8, lanes), jnp.float32)
    sums = lax.fori_loop(0, half // LINES, line, ((zero,) * 6,) * grid_y)
    for i in range(half // LINES * LINES, half):
        sums = tuple(one_line(j, i, sums[j]) for j in range(grid_y))
    measure_peaks(grid_x, grid_y, length, peaks, valid, sums, group, mine, score)
    sweep(grid_x, grid_y, float(length // 2), mine, moved, inbox, grid, sweep_send, sweep_recv)

    def sent(part, carry):
        for dx, dy in SIDES:

            @pl.when(inside(dx, dy))
            def _():
                copy(dx, dy, part).wait_send()

        return carry

    lax.fori_loop(0, PARTS, sent, 0)


def body(volumes, peaks, valid):
    length = volumes.shape[1]
    margin = length // 4
    half = length // 2 + 1
    _, grid_y, grid_x = peaks.shape
    lanes = grid_x * length
    tall, own = volumes.shape[2:]
    height = tall + 2 * margin
    table_x, table_y, table_z = tables(length, grid_x, grid_y)
    far_x, far_y = reach_of(grid_x, grid_y)
    deep = -(-(2 * far_y + 1) * grid_y // 8) * 8
    wide = -(-(2 * far_x + 1) * grid_x // 128) * 128
    lines = -(-half // 8) * 8
    count = len(partners(grid_x, grid_y))
    vmem = pl.BlockSpec(memory_space=pltpu.VMEM)
    smem = pl.BlockSpec(memory_space=pltpu.SMEM)
    return pl.pallas_call(
        functools.partial(spectrum_kernel, grid_x, grid_y),
        out_shape=(
            jax.ShapeDtypeStruct(peaks.shape, jnp.float32),
            jax.ShapeDtypeStruct(valid.shape, jnp.float32),
        ),
        in_specs=[vmem] * 6 + [smem] * 2,
        out_specs=(vmem, vmem),
        scratch_shapes=[
            pltpu.VMEM((grid_y, grid_x * 8, 2 * length), jnp.bfloat16),
            pltpu.VMEM((grid_y, 3, lines, lanes), jnp.float32),
            pltpu.VMEM((grid_y, 3, lines, lanes), jnp.float32),
            pltpu.VMEM((2, length, height, 2 * lanes), jnp.bfloat16),
            pltpu.VMEM((2 * lanes // 128, table_y.shape[0] // 2 * PITCH, 128), jnp.float32),
            pltpu.VMEM((2, length // GROUP, 2, tall, GROUP * margin), jnp.bfloat16),
            pltpu.VMEM((2, 2, length, margin, own), jnp.bfloat16),
            pltpu.VMEM((2, length // GROUP, 2, height, GROUP * margin), jnp.bfloat16),
            pltpu.VMEM((2, length, height, own), jnp.bfloat16),
            pltpu.SemaphoreType.DMA((len(SIDES), PARTS)),
            pltpu.SemaphoreType.DMA((len(SIDES), PARTS)),
            pltpu.VMEM((4 * grid_y, wide), jnp.float32),
            pltpu.VMEM((count, 4 * grid_y, wide), jnp.float32),
            pltpu.VMEM((4, deep, wide), jnp.float32),
            pltpu.SemaphoreType.DMA((count,)),
            pltpu.SemaphoreType.DMA((count,)),
        ],
        compiler_params=pltpu.CompilerParams(
            vmem_limit_bytes=60 * 1024 * 1024, collective_id=0, has_side_effects=True
        ),
        name="correlate",
    )(volumes, *strip_tables(margin, own), table_x, table_y, table_z, peaks, valid)


def solution(mesh):
    return jax.shard_map(
        body,
        mesh=mesh,
        in_specs=(P(None, None, "gy", "gx"), P(None, "gy", "gx"), P("gy", "gx")),
        out_specs=(P(None, "gy", "gx"), P("gy", "gx")),
        check_vma=False,
    )
```

time: 165 us -> 52.5 us (0.32)
  starting transfers between devices: 42 us -> 0 us
  waiting for transfers between devices: 38.6 us -> 0 us
  other arithmetic: 14.9 us -> 0 us
  local copies, waits for them, and re-layouts: 17.2 us -> 2.47 us
    ppermute x16 -> x0, starting transfers between devices: 42 us -> none  [the longest x8 28.3 us: padded_2(): before = lax.ppermute(last, axis, up)]
    ppermute x16 -> x0, waiting for transfers between devices: 38.6 us -> none  [the longest x8 20.5 us: padded_2(): after = lax.ppermute(initial, axis, down)]
    concatenate x7 -> x0, other arithmetic: 9.18 us -> none  [padded_2(): array = jnp.concatenate([before, array, after], axis=dim)]
    slice x8 -> x0, local copies, waits for them, and re-layouts: 4.7 us -> none  [the longest x4 4.67 us: padded_2(): last = lax.slice_in_dim(array, length - width, length, axis=dim)]
    ppermute x2 -> x0, local copies, waits for them, and re-layouts: 4.4 us -> none  [the longest x1 2.64 us: padded_2(): before = lax.ppermute(last, axis, up)]
    reshape x6 -> x0, local copies, waits for them, and re-layouts: 3.68 us -> none  [the longest x4 2.06 us: spread(): return table.reshape(grid_y, 3, half, lanes)]
    slice x2 -> x0, other arithmetic: 3.13 us -> none  [the longest x1 2.87 us: padded_2(): last = lax.slice_in_dim(array, length - width, length, axis=dim)]
    unnamed x18 -> x2, local copies, waits for them, and re-layouts: 3.55 us -> 2.47 us
  transfers between devices with their start and end apart: 16 -> 0, of which waited for: 10 -> 0; matrix products, arithmetic and copies ran while one was open for 5% -> 0% of each run, Pallas kernels for 0% -> 0%
where the time goes in v3:
time: 52.5 us; the launch traced here: 52 us
  Pallas kernels  48.9 us (93%)
  local copies, waits for them, and re-layouts  2.47 us (5%)
  between operations  0.64 us (1%)
    pallas_call x1, Pallas kernels, body(): pl.pallas_call(functools.partial(spectrum_kernel, grid_x, grid_y), out_sh...  48.9 us
    unnamed x2, local copies, waits for them, and re-layouts  2.47 us

profile of v3, /device:TPU:4, one launch (start us, length us, event | category | flops | bytes accessed | tf_op | source)
XLA Modules:
  0.0 52.0 jit_solution(3764629507221505186)
XLA Ops:
  0.6 48.9 %correlate.1 = (f32[3,2,4]{2,1,0:T(2,128)}, f32[2,4]{1,0:T(2,128)}) custom-call(bf16[2,64,64,128]{3,2,1,0:T(8,128)(2,1)} %vol.1, bf16[1024,256]{1,0:T(8,128)(2,1)} %constant.10.clone.pack, bf16[256,1024]{1,0:T(8,128)(2,1)} %constant.11.clone.unpack, bf16[256,512]{1,0:T(8,128)(2,1)} %constant.12.clone.table_x, bf16[144,192]{1,0:T(8,128)(2,1)} %constant.13.clone.table_y, ...), custom_call_target="tpu_custom_call" | custom-call | tf_op jit(solution)/shard_map/correlate/pallas_call | solution.py:560
  49.6 1.3 %copy.12 = f32[3,2,4]{2,1,0:T(2,128)} copy(f32[3,2,4]{2,1,0:T(2,128)} %get-tuple-element.4) | data formatting | bytes 192
  50.8 1.2 %copy.13 = f32[2,4]{1,0:T(2,128)} copy(f32[2,4]{1,0:T(2,128)} %get-tuple-element.5) | data formatting | bytes 64

commit v4 on v3

--- a/solution.py
+++ b/solution.py
@@ -15,7 +15,7 @@
 LINES = 3
 
 
-PARTS = 4
+PARTS = 8
 GROUP = 8
 PITCH = 136
 SIDES = [(dx, dy) for dy in (-1, 0, 1) for dx in (-1, 0, 1) if (dx, dy) != (0, 0)]
@@ -248,7 +248,7 @@
         table_e[j] = jnp.where(outer == inner, cosine, signed).astype(jnp.bfloat16)
 
 
-def measure_peaks(grid_x, grid_y, length, peaks, valid, sums, group, mine, score):
+def measure_peaks(grid_x, grid_y, length, peaks, valid, sums, group, mine, out):
     lanes = group.shape[1]
     wide = mine.shape[1]
     k = lax.broadcasted_iota(jnp.int32, (8, lanes), 1) & (length - 1)
@@ -289,7 +289,7 @@
         for c in range(3):
             mine[c * grid_y + j : c * grid_y + j + 1, :] = data[c : c + 1]
         mine[3 * grid_y + j : 3 * grid_y + j + 1, :] = trust[:1]
-        score[j : j + 1, :] = centre[:, :grid_x]
+        out[3, j : j + 1, :] = centre[:, :grid_x]
 
 
 def spectrum_kernel(
@@ -304,7 +304,6 @@
     peaks,
     valid,
     moved,
-    score,
     table_e,
     cos_y,
     sin_y,
@@ -526,7 +525,7 @@
     sums = lax.fori_loop(0, half // LINES, line, ((zero,) * 6,) * grid_y)
     for i in range(half // LINES * LINES, half):
         sums = tuple(one_line(j, i, sums[j]) for j in range(grid_y))
-    measure_peaks(grid_x, grid_y, length, peaks, valid, sums, group, mine, score)
+    measure_peaks(grid_x, grid_y, length, peaks, valid, sums, group, mine, moved)
     sweep(grid_x, grid_y, float(length // 2), mine, moved, inbox, grid, sweep_send, sweep_recv)
 
     def sent(part, carry):
@@ -557,14 +556,11 @@
     count = len(partners(grid_x, grid_y))
     vmem = pl.BlockSpec(memory_space=pltpu.VMEM)
     smem = pl.BlockSpec(memory_space=pltpu.SMEM)
-    return pl.pallas_call(
+    result = pl.pallas_call(
         functools.partial(spectrum_kernel, grid_x, grid_y),
-        out_shape=(
-            jax.ShapeDtypeStruct(peaks.shape, jnp.float32),
-            jax.ShapeDtypeStruct(valid.shape, jnp.float32),
-        ),
+        out_shape=jax.ShapeDtypeStruct((4, grid_y, grid_x), jnp.float32),
         in_specs=[vmem] * 6 + [smem] * 2,
-        out_specs=(vmem, vmem),
+        out_specs=vmem,
         scratch_shapes=[
             pltpu.VMEM((grid_y, grid_x * 8, 2 * length), jnp.bfloat16),
             pltpu.VMEM((grid_y, 3, lines, lanes), jnp.float32),
@@ -588,6 +584,7 @@
         ),
         name="correlate",
     )(volumes, *strip_tables(margin, own), table_x, table_y, table_z, peaks, valid)
+    return (result[:3], result[3])
 
 
 def solution(mesh):

time: 52.5 us -> 53.4 us (1.017)
    unnamed x2 -> x0, local copies, waits for them, and re-layouts: 2.47 us -> none
    slice x0 -> x1, local copies, waits for them, and re-layouts: none -> 1.26 us  [body(): return (result[:3], result[3])]
    squeeze x0 -> x1, local copies, waits for them, and re-layouts: none -> 1.22 us  [body(): return (result[:3], result[3])]
where the time goes in v4:
time: 53.4 us; the launch traced here: 52.5 us
  Pallas kernels  49.4 us (93%)
  local copies, waits for them, and re-layouts  2.48 us (5%)
  between operations  0.64 us (1%)
    pallas_call x1, Pallas kernels, body(): pl.pallas_call(functools.partial(spectrum_kernel, grid_x, grid_y), out_sh...  49.4 us
    slice x1, local copies, waits for them, and re-layouts, body(): return (result[:3], result[3])  1.26 us
    squeeze x1, local copies, waits for them, and re-layouts, body(): return (result[:3], result[3])  1.22 us

profile of v4, /device:TPU:4, one launch (start us, length us, event | category | flops | bytes accessed | tf_op | source)
XLA Modules:
  0.0 52.5 jit_solution(16586324714812203132)
XLA Ops:
  0.6 49.4 %correlate.1 = f32[4,2,4]{2,1,0:T(2,128)} custom-call(bf16[2,64,64,128]{3,2,1,0:T(8,128)(2,1)} %vol.1, bf16[1024,256]{1,0:T(8,128)(2,1)} %constant.10.clone.pack, bf16[256,1024]{1,0:T(8,128)(2,1)} %constant.11.clone.unpack, bf16[256,512]{1,0:T(8,128)(2,1)} %constant.12.clone.table_x, bf16[144,192]{1,0:T(8,128)(2,1)} %constant.13.clone.table_y, ...), custom_call_target="tpu_custom_call" | custom-call | tf_op jit(solution)/shard_map/correlate/pallas_call | solution.py:559
  50.1 1.2 %slice_bitcast_fusion = f32[2,4]{1,0:T(2,128)} fusion(f32[4,2,4]{2,1,0:T(2,128)} %correlate.1), kind=kLoop, calls=%fused_computation | loop fusion | bytes 64 | tf_op jit(solution)/shard_map/squeeze | solution.py:587
  51.3 1.3 %slice.6 = f32[3,2,4]{2,1,0:T(2,128)} slice(f32[4,2,4]{2,1,0:T(2,128)} %correlate.1), slice={[0:3], [0:2], [0:4]} | slice | bytes 192 | tf_op jit(solution)/shard_map/slice | solution.py:587
